TPU v7x, 128 devices: a whole 4x4x4 slice. The times are simulated.
128 devices in a mesh: lev: 8 (over y, core), row: 16 (over z, x).
Axes of the slice: x: 4, y: 4, z: 4, core: 2. Of those that a mesh axis runs over, the one named last changes fastest.
Arguments:
- tracer: float32 [128, 64, 4096], P('lev', 'row'), may hold values from -6 to 6
- courant_x: float32 [128, 64, 4096], P('lev', 'row'), may hold values from 0.05 to 0.45
- courant_y: float32 [128, 64, 4096], P('lev', 'row'), may hold values from 0.05 to 0.45
- wind_x: int32 [128, 64, 4096], P('lev', 'row'), may hold values 0 or 1
- wind_y: int32 [128, 64, 4096], P('lev', 'row'), may hold values 0 or 1
- inverse_diffusion: float32 [4096, 128, 128], P(('lev', 'row')), may hold values from -0.5 to 1.5
- receptor_cell: int32 [262144], P(('lev', 'row')), may hold values from 0 to 262143
- receptor_limit: float32 [262144], P(('lev', 'row')), may hold values from -1 to 1
- stack_cell: int32 [65536], P(('lev', 'row')), may hold values from 0 to 262143
- stack_dest: int32 [65536, 1], P(('lev', 'row')), may hold values from 0 to 127; in each aligned block of 512 rows (0 to 511, 512 to 1023, ...) at most 12 rows name the same one
- stack_slot: int32 [65536], P(('lev', 'row')), may hold values from 0 to 255
- stack_weight: float32 [65536], P(('lev', 'row')), may hold values from 0.5 to 2
Outputs:
- final_field: float32 [4096, 64, 128], P(('lev', 'row'))
- crossing: float32 [262144], P(('lev', 'row'))
- adjoint_init: float32 [128, 64, 4096], P('lev', 'row')
- inventory_grad: float32 [32768], P(('lev', 'row'))
Inputs may be any that keep to these rules, and one draw needn't show every extreme that they name: `stack_dest`: among the stacks of one slab strip at most 12 have the same owner.
All inputs are finite; a program needn't handle non-finite values. No bound on the sum of `wind_x` or of `wind_y` on one device may be relied on, other than what follows from the above.
Results may differ from a plain program's by a relative error of at most 0.00011.
Values sent between devices are 32-bit elements; how exact they have to be, the bound alone decides.
A program may use at most 128 MiB of HBM per device.

v0:
```python
import jax
import jax.numpy as jnp
from jax import lax
from jax.sharding import PartitionSpec as P

INV_DEV = 256


SHARPNESS = 2.0


def with_halo(shard, sides, width):
    for axis, dim in sides:
        count, length = (lax.axis_size(axis), shard.shape[dim])
        up = [(i, (i + 1) % count) for i in range(count - 1)]
        down = [(j, i) for i, j in up]
        last = lax.slice_in_dim(shard, length - width, length, axis=dim)
        initial = lax.slice_in_dim(shard, 0, width, axis=dim)
        before = lax.ppermute(last, axis, up)
        after = lax.ppermute(initial, axis, down)
        shard = jnp.concatenate([before, shard, after], axis=dim)
    return shard


def advect(field, courant_x, courant_y, sign_x, sign_y):
    padded = with_halo(field, (("row", 1),), 1)
    lower_x = padded[:, :-2]
    upper_x = padded[:, 2:]
    zero_col = jnp.zeros(field.shape[:2] + (1,), jnp.float32)
    lower_y = jnp.concatenate([zero_col, field[:, :, :-1]], 2)
    upper_y = jnp.concatenate([field[:, :, 1:], zero_col], 2)
    return (
        (1.0 - courant_x - courant_y) * field
        + courant_x * (sign_x * lower_x + (1.0 - sign_x) * upper_x)
        + courant_y * (sign_y * lower_y + (1.0 - sign_y) * upper_y)
    )


def adjoint_advect(back, courant_x, courant_y, sign_x, sign_y):
    toward_lower = courant_x * sign_x * back
    toward_upper = courant_x * (1.0 - sign_x) * back
    edge_rows = jnp.concatenate([toward_lower[:, :1], toward_upper[:, 1:]], 1)
    padded = with_halo(edge_rows, (("row", 1),), 1)
    from_above = jnp.concatenate([toward_lower[:, 1:], padded[:, -1:]], 1)
    from_below = jnp.concatenate([padded[:, :1], toward_upper[:, :-1]], 1)
    left_flux = courant_y * sign_y * back
    right_flux = courant_y * (1.0 - sign_y) * back
    zero_col = jnp.zeros(back.shape[:2] + (1,), jnp.float32)
    from_right = jnp.concatenate([left_flux[:, :, 1:], zero_col], 2)
    from_left = jnp.concatenate([zero_col, right_flux[:, :, :-1]], 2)
    return (1.0 - courant_x - courant_y) * back + from_above + from_below + from_right + from_left


def to_columns(slab):
    received = lax.all_to_all(
        lax.all_to_all(slab, "lev", split_axis=2, concat_axis=0, tiled=True),
        "row",
        split_axis=2,
        concat_axis=1,
        tiled=True,
    )
    return jnp.transpose(received, (2, 1, 0))


def to_slabs(pencil, num_lev, num_row):
    block_y, all_rows, all_levels = pencil.shape
    slab_levels = all_levels // num_lev
    strip_rows = all_rows // num_row
    flipped = jnp.transpose(pencil, (2, 1, 0))
    received = lax.all_to_all(
        lax.all_to_all(flipped, "lev", split_axis=0, concat_axis=2, tiled=True),
        "row",
        split_axis=1,
        concat_axis=2,
        tiled=True,
    )
    received = received.reshape(slab_levels, strip_rows, num_row, num_lev, block_y)
    return jnp.transpose(received, (0, 1, 3, 2, 4)).reshape(
        slab_levels, strip_rows, num_lev * num_row * block_y
    )


def local(
    tracer,
    courant_x,
    courant_y,
    wind_x,
    wind_y,
    inverse_diffusion,
    receptor_cell,
    receptor_limit,
    stack_cell,
    stack_dest,
    stack_slot,
    stack_weight,
):
    num_lev = lax.axis_size("lev")
    num_row = lax.axis_size("row")
    devices = num_lev * num_row
    sign_x = wind_x.astype(jnp.float32)
    sign_y = wind_y.astype(jnp.float32)
    advected = advect(tracer, courant_x, courant_y, sign_x, sign_y)
    columns = to_columns(advected)
    final_field = jnp.einsum(
        "yxk,ylk->yxl", columns, inverse_diffusion, precision=lax.Precision.HIGHEST
    )
    picked = final_field.reshape(-1)[receptor_cell]
    crossing = jax.nn.sigmoid(SHARPNESS * (picked - receptor_limit))
    seed_terms = SHARPNESS * crossing * (1.0 - crossing)
    seed_field = (
        jnp.zeros((final_field.size,), jnp.float32)
        .at[receptor_cell]
        .add(seed_terms)
        .reshape(final_field.shape)
    )
    back_mid = jnp.einsum(
        "yxl,ylk->yxk", seed_field, inverse_diffusion, precision=lax.Precision.HIGHEST
    )
    back_slab = to_slabs(back_mid, num_lev, num_row)
    adjoint_init = adjoint_advect(back_slab, courant_x, courant_y, sign_x, sign_y)
    stack_values = stack_weight * adjoint_init.reshape(-1)[stack_cell]
    owner_device = stack_dest[:, 0]
    partial_grad = (
        jnp.zeros((devices * INV_DEV,), jnp.float32)
        .at[owner_device * INV_DEV + stack_slot]
        .add(stack_values)
    )
    inventory_grad = lax.psum_scatter(partial_grad, ("lev", "row"), scatter_dimension=0, tiled=True)
    return (final_field, crossing, adjoint_init, inventory_grad)


def solution(mesh):
    return jax.shard_map(
        local,
        mesh=mesh,
        in_specs=(
            P("lev", "row", None),
            P("lev", "row", None),
            P("lev", "row", None),
            P("lev", "row", None),
            P("lev", "row", None),
            P(("lev", "row"), None, None),
            P(("lev", "row")),
            P(("lev", "row")),
            P(("lev", "row")),
            P(("lev", "row"), None),
            P(("lev", "row")),
            P(("lev", "row")),
        ),
        out_specs=(
            P(("lev", "row"), None, None),
            P(("lev", "row")),
            P("lev", "row", None),
            P(("lev", "row")),
        ),
        check_vma=False,
    )
```

profile of v0, /device:TPU:1, one launch (start us, length us, event | category | flops | bytes accessed | tf_op | source)
XLA Modules:
  0.0 380.2 jit_solution(9905332777434923256)
XLA Ops:
  7.2 2.0 copy.76
  10.6 4.9 %collective-permute-start = (f32[16,1,4096]{2,0,1:T(8,128)S(1)}, f32[16,1,4096]{2,0,1:T(8,128)S(1)}, u32[]{:S(2)}, u32[]{:S(2)}) collective-permute-start(f32[16,1,4096]{2,0,1:T(8,128)S(1)} %get-tuple-element.27), channel_id=1, source_target_pairs={{0,1},{1,2},{2,3},{3,4},{4,5},{5,6},{6,7},{7,8},{8,9},{9,10},{10,1... | collective-permute-start | bytes 786440 | tf_op jit(solution)/shard_map/ppermute | solution.py:19
  15.8 2.9 collective-permute-done.1
  19.9 4.1 %fusion.13 = (f32[16,4,4096]{2,0,1:T(8,128)}, f32[16,4,4096]{2,0,1:T(8,128)S(1)}, f32[16,4,4096]{2,0,1:T(8,128)}) fusion(f32[16,4,4096]{2,1,0:T(4,128)S(1)} %copy-done.11, f32[16,4,4095]{2,0,1:T(8,128)S(1)} %get-tuple-element.26, f32[16,4,4095]{2,0,1:T(8,128)S(1)} %get-tuple-element.25, s32[16,4,4096]{2,1,0:T(4,128)S(1)} %copy-done.8, ...), kind=kLoop, calls=%fused_computation.39 | loop fusion | flops 4980736 | bytes 11009536 | tf_op args[2]
  24.0 5.9 %copy.87 = f32[16,4,4096]{0,1,2:T(4,128)} copy(f32[16,4,4096]{2,0,1:T(8,128)S(1)} %get-tuple-element.23) | data formatting | bytes 2097152 | tf_op jit(solution)/shard_map/add | solution.py:33
  29.9 9.3 %reshape.71 = f32[8,1,32768]{2,1,0:T(1,128)S(1)} reshape(f32[4096,4,16]{2,1,0:T(4,128)} %bitcast.43) | data formatting | bytes 2097152
  39.2 22.2 %all_to_all.69 = f32[8,1,32768]{2,1,0:T(1,128)} all-to-all(f32[8,1,32768]{2,1,0:T(1,128)S(1)} %reshape.71), channel_id=1, replica_groups=mesh['lev'=8,'row'=16] {'lev'}, dimensions={0} | all-to-all | bytes 2097152 | tf_op jit(solution)/shard_map/all_to_all | solution.py:56
  62.0 4.4 %reduce = f32[8,32768]{1,0:T(8,128)S(1)} reduce(f32[8,1,32768]{2,1,0:T(1,128)} %all_to_all.69, f32[]{:T(128)} %broadcast.63), dimensions={1}, to_apply=%all_to_all.50.reduce_sub_computation | reduce | bytes 2097156 | tf_op jit(solution)/shard_map/all_to_all | solution.py:56
  66.3 9.0 %reshape.72 = f32[4096,4,16]{2,1,0:T(4,128)} reshape(f32[8,32768]{1,0:T(8,128)S(1)} %reduce) | data formatting | bytes 2097152
  75.3 6.7 %copy.105 = f32[16,4,8,512]{3,0,2,1:T(8,128)S(1)} copy(f32[16,4,8,512]{0,1,3,2:T(4,128)} %bitcast.44) | data formatting | bytes 2097152 | tf_op jit(solution)/shard_map/all_to_all | solution.py:56
  83.3 10.5 %all-to-all-start.1 = ((f32[128,4,512]{0,1,2:T(4,128)}), f32[128,4,512]{0,1,2:T(4,128)S(1)}, u32[]{:S(2)}, u32[]{:S(2)}) async-start(f32[128,4,512]{0,1,2:T(4,128)} %copy.90), calls=%async_computation.1 | async-start | bytes 2097152 | tf_op jit(solution)/shard_map/all_to_all | solution.py:55
  93.8 15.6 %all-to-all-done.1 = f32[128,4,512]{0,1,2:T(4,128)S(1)} async-done(((f32[128,4,512]{0,1,2:T(4,128)}), f32[128,4,512]{0,1,2:T(4,128)S(1)}, u32[]{:S(2)}, u32[]{:S(2)}) %all-to-all-start.1) | async-done | bytes 1048608 | tf_op jit(solution)/shard_map/all_to_all | solution.py:55
  110.2 4.1 %fusion.16 = f32[32,64,128]{2,1,0:T(8,128)S(1)} fusion(f32[32,64,128]{2,1,0:T(8,128)S(1)} %bitcast.55, f32[32,128,128]{2,1,0:T(8,128)S(1)} %copy-done), kind=kOutput, calls=%fused_computation.42 | convolution fusion | flops 402653184 | bytes 4194304 | tf_op jit(solution)/shard_map/yxk,ylk->yxl/dot_general | solution.py:104
  114.4 11.8 %gather_fusion = f32[2048]{0:T(1024)S(1)} fusion(f32[262144]{0:T(1024)S(1)} %bitcast.42, s32[2048]{0:T(1024)S(1)} %get-tuple-element.30), kind=kCustom, calls=%fused_computation | custom fusion | bytes 24576 | tf_op jit(solution)/shard_map/gather | solution.py:107
  126.8 12.3 %scatter_custom_fusion = f32[262144]{0:T(1024)} fusion(s32[2048]{0:T(1024)S(1)} %get-tuple-element.29, f32[2048]{0:T(1024)S(1)} %get-tuple-element.16, f32[]{:T(128)} %constant.8.clone.1), kind=kCustom, calls=%fused_computation.26 | custom fusion | flops 2048 | bytes 1048580 | tf_op jit(solution)/shard_map/scatter-add | solution.py:113
  139.1 3.2 convolution_bitcast_fusion
  144.2 2.1 reshape.73
  146.3 6.6 %all-to-all-start.2 = ((f32[8,1,32768]{2,1,0:T(1,128)}), f32[8,1,32768]{2,1,0:T(1,128)S(1)}, u32[]{:S(2)}, u32[]{:S(2)}) async-start(f32[8,1,32768]{2,1,0:T(1,128)} %reshape.73), calls=%async_computation.2 | async-start | bytes 2097152 | tf_op jit(solution)/shard_map/all_to_all | solution.py:71
  153.0 15.0 %all-to-all-done.2 = f32[8,1,32768]{2,1,0:T(1,128)S(1)} async-done(((f32[8,1,32768]{2,1,0:T(1,128)}), f32[8,1,32768]{2,1,0:T(1,128)S(1)}, u32[]{:S(2)}, u32[]{:S(2)}) %all-to-all-start.2) | async-done | bytes 1048608 | tf_op jit(solution)/shard_map/all_to_all | solution.py:71
  168.0 3.1 reduce.1
  173.5 3.5 copy.95
  177.0 3.7 all-to-all-start.3
  182.3 14.4 %all-to-all-done.3 = f32[16,64,256]{2,0,1:T(8,128)S(1)} async-done(((f32[16,64,256]{2,0,1:T(8,128)}), f32[16,64,256]{2,0,1:T(8,128)S(1)}, u32[]{:S(2)}, u32[]{:S(2)}) %all-to-all-start.3) | async-done | bytes 1048608 | tf_op jit(solution)/shard_map/all_to_all | solution.py:70
  197.3 2.4 reshape.28
  199.8 5.1 %copy.97 = f32[16,4,8,16,32]{4,3,2,0,1:T(8,128)} copy(f32[16,4,8,16,32]{4,2,3,1,0:T(8,128)} %bitcast.45) | data formatting | bytes 2097152 | tf_op jit(solution)/shard_map/transpose | solution.py:78
  204.9 3.6 reshape.29
  208.5 2.7 multiply_multiply_fusion
  212.6 4.3 %collective-permute-start.3 = (f32[16,1,4096]{2,0,1:T(8,128)S(1)}, f32[16,1,4096]{2,0,1:T(8,128)S(1)}, u32[]{:S(2)}, u32[]{:S(2)}) collective-permute-start(f32[16,1,4096]{2,0,1:T(8,128)S(1)} %slice.62), channel_id=1, source_target_pairs={{0,1},{1,2},{2,3},{3,4},{4,5},{5,6},{6,7},{7,8},{8,9},{9,10},{10,1... | collective-permute-start | bytes 786440 | tf_op jit(solution)/shard_map/ppermute | solution.py:19
  222.5 3.1 gather_fusion.1
  225.7 3.9 %scatter_custom_fusion.1 = f32[32768]{0:T(1024)} fusion(s32[512]{0:T(512)S(1)} %compare_select_fusion.2, f32[512]{0:T(512)S(1)} %mul.91, f32[]{:T(128)} %constant.8.clone.1), kind=kCustom, calls=%fused_computation.29 | custom fusion | flops 512 | bytes 131076 | tf_op jit(solution)/shard_map/scatter-add | solution.py:126
  229.6 2.9 copy.103
  232.5 139.3 %all-reduce.7.cloned.1.call-done = f32[32768]{0:T(1024)} async-done(((f32[32768]{0:T(1024)}), f32[32768]{0:T(1024)}) %all-reduce.7.cloned.1.call-update) | async-done | bytes 131088
  (74 shorter events, 20.9 us)
Async XLA Ops:
  7.2 103.0 %copy-start = (f32[32,128,128]{2,1,0:T(8,128)S(1)}, f32[32,128,128]{2,1,0:T(8,128)}, u32[]{:S(2)}) copy-start(f32[32,128,128]{2,1,0:T(8,128)} %param.17) | copy-start | bytes 6291460
  9.2 9.5 %collective-permute-start.1 = (f32[16,1,4096]{2,0,1:T(8,128)S(1)}, f32[16,1,4096]{2,0,1:T(8,128)S(1)}, u32[]{:S(2)}, u32[]{:S(2)}) collective-permute-start(f32[16,1,4096]{2,0,1:T(8,128)S(1)} %get-tuple-element.28), channel_id=1, source_target_pairs={{1,0},{2,1},{3,2},{4,3},{5,4},{6,5},{7,6},{8,7},{9,8},{10,9},{11,1... | collective-permute-start | bytes 786440 | tf_op jit(solution)/shard_map/ppermute | solution.py:20
  10.5 9.4 %copy-start.4 = (f32[16,4,4096]{2,1,0:T(4,128)S(1)}, f32[16,4,4096]{2,1,0:T(4,128)}, u32[]{:S(2)}) copy-start(f32[16,4,4096]{2,1,0:T(4,128)} %param.13) | copy-start | bytes 3145732
  10.5 9.3 %copy-start.7 = (s32[16,4,4096]{2,1,0:T(4,128)S(1)}, s32[16,4,4096]{2,1,0:T(4,128)}, u32[]{:S(2)}) copy-start(s32[16,4,4096]{2,1,0:T(4,128)} %param.15) | copy-start | bytes 3145732
  10.5 9.3 %copy-start.8 = (s32[16,4,4096]{2,1,0:T(4,128)S(1)}, s32[16,4,4096]{2,1,0:T(4,128)}, u32[]{:S(2)}) copy-start(s32[16,4,4096]{2,1,0:T(4,128)} %param.16) | copy-start | bytes 3145732
  10.5 9.3 %copy-start.11 = (f32[16,4,4096]{2,1,0:T(4,128)S(1)}, f32[16,4,4096]{2,1,0:T(4,128)}, u32[]{:S(2)}) copy-start(f32[16,4,4096]{2,1,0:T(4,128)} %param.14) | copy-start | bytes 3145732
  10.6 9.3 %collective-permute-start = (f32[16,1,4096]{2,0,1:T(8,128)S(1)}, f32[16,1,4096]{2,0,1:T(8,128)S(1)}, u32[]{:S(2)}, u32[]{:S(2)}) collective-permute-start(f32[16,1,4096]{2,0,1:T(8,128)S(1)} %get-tuple-element.27), channel_id=1, source_target_pairs={{0,1},{1,2},{2,3},{3,4},{4,5},{5,6},{6,7},{7,8},{8,9},{9,10},{10,1... | collective-permute-start | bytes 786440 | tf_op jit(solution)/shard_map/ppermute | solution.py:19
  82.0 11.8 %copy-start.14 = (s32[2048]{0:T(1024)S(1)}, s32[2048]{0:T(1024)}, u32[]{:S(2)}) copy-start(s32[2048]{0:T(1024)} %param.18) | copy-start | bytes 24580
  83.3 26.1 %all-to-all-start.1 = ((f32[128,4,512]{0,1,2:T(4,128)}), f32[128,4,512]{0,1,2:T(4,128)S(1)}, u32[]{:S(2)}, u32[]{:S(2)}) async-start(f32[128,4,512]{0,1,2:T(4,128)} %copy.90), calls=%async_computation.1 | async-start | bytes 2097152 | tf_op jit(solution)/shard_map/all_to_all | solution.py:55
  114.3 11.8 %copy-start.2 = (f32[32,64,128]{2,1,0:T(8,128)}, f32[32,64,128]{2,1,0:T(8,128)S(1)}, u32[]{:S(2)}) copy-start(f32[32,64,128]{2,1,0:T(8,128)S(1)} %fusion.16) | copy-start | bytes 3145732
  114.3 11.8 %copy-start.15 = (f32[2048]{0:T(1024)S(1)}, f32[2048]{0:T(1024)}, u32[]{:S(2)}) copy-start(f32[2048]{0:T(1024)} %param.19) | copy-start | bytes 24580
  144.1 8.8 %copy-start.18 = (s32[512,1]{0,1:T(1,128)S(1)}, s32[512,1]{0,1:T(1,128)}, u32[]{:S(2)}) copy-start(s32[512,1]{0,1:T(1,128)} %param.21) | copy-start | bytes 6148
  144.1 8.8 %copy-start.19 = (s32[512]{0:T(512)S(1)}, s32[512]{0:T(512)}, u32[]{:S(2)}) copy-start(s32[512]{0:T(512)} %param.20) | copy-start | bytes 6148
  144.2 8.8 %copy-start.16 = (s32[512]{0:T(512)S(1)}, s32[512]{0:T(512)}, u32[]{:S(2)}) copy-start(s32[512]{0:T(512)} %param.22) | copy-start | bytes 6148
  146.3 21.7 %all-to-all-start.2 = ((f32[8,1,32768]{2,1,0:T(1,128)}), f32[8,1,32768]{2,1,0:T(1,128)S(1)}, u32[]{:S(2)}, u32[]{:S(2)}) async-start(f32[8,1,32768]{2,1,0:T(1,128)} %reshape.73), calls=%async_computation.2 | async-start | bytes 2097152 | tf_op jit(solution)/shard_map/all_to_all | solution.py:71
  173.5 7.2 %copy-start.9 = (s32[16,4,4096]{2,1,0:T(4,128)S(1)}, s32[16,4,4096]{2,1,0:T(4,128)}, u32[]{:S(2)}) copy-start(s32[16,4,4096]{2,1,0:T(4,128)} %param.16) | copy-start | bytes 3145732
  177.0 19.7 %all-to-all-start.3 = ((f32[16,64,256]{2,0,1:T(8,128)}), f32[16,64,256]{2,0,1:T(8,128)S(1)}, u32[]{:S(2)}, u32[]{:S(2)}) async-start(f32[16,64,256]{2,0,1:T(8,128)} %copy.95), calls=%async_computation.3 | async-start | bytes 2097152 | tf_op jit(solution)/shard_map/all_to_all | solution.py:70
  180.7 191.1 %all-reduce.7.cloned.1.call-start = ((), (), s32[]{:S(2)}) async-start(), calls=%async_computation.4 | async-start | bytes 262144
  204.9 3.6 copy-start.5
  208.5 8.3 %copy-start.6 = (f32[16,4,4096]{2,0,1:T(8,128)S(1)}, f32[16,4,4096]{2,0,1:T(8,128)}, u32[]{:S(2)}) copy-start(f32[16,4,4096]{2,0,1:T(8,128)} %get-tuple-element.22) | copy-start | bytes 3145732
  208.5 8.3 %copy-start.10 = (f32[16,4,4096]{2,0,1:T(8,128)S(1)}, f32[16,4,4096]{2,0,1:T(8,128)}, u32[]{:S(2)}) copy-start(f32[16,4,4096]{2,0,1:T(8,128)} %copy_convert_fusion) | copy-start | bytes 3145732
  208.5 8.3 %copy-start.13 = (f32[16,4,4096]{2,0,1:T(8,128)S(1)}, f32[16,4,4096]{2,0,1:T(8,128)}, u32[]{:S(2)}) copy-start(f32[16,4,4096]{2,0,1:T(8,128)} %get-tuple-element.24) | copy-start | bytes 3145732
  211.3 7.1 %collective-permute-start.2 = (f32[16,1,4096]{2,0,1:T(8,128)S(1)}, f32[16,1,4096]{2,0,1:T(8,128)S(1)}, u32[]{:S(2)}, u32[]{:S(2)}) collective-permute-start(f32[16,1,4096]{2,0,1:T(8,128)S(1)} %slice.61), channel_id=1, source_target_pairs={{1,0},{2,1},{3,2},{4,3},{5,4},{6,5},{7,6},{8,7},{9,8},{10,9},{11,1... | collective-permute-start | bytes 786440 | tf_op jit(solution)/shard_map/ppermute | solution.py:20
  212.6 7.3 %collective-permute-start.3 = (f32[16,1,4096]{2,0,1:T(8,128)S(1)}, f32[16,1,4096]{2,0,1:T(8,128)S(1)}, u32[]{:S(2)}, u32[]{:S(2)}) collective-permute-start(f32[16,1,4096]{2,0,1:T(8,128)S(1)} %slice.62), channel_id=1, source_target_pairs={{0,1},{1,2},{2,3},{3,4},{4,5},{5,6},{6,7},{7,8},{8,9},{9,10},{10,1... | collective-permute-start | bytes 786440 | tf_op jit(solution)/shard_map/ppermute | solution.py:19
  217.8 2.0 copy-start.12
  221.4 1.0 copy-start.3
  222.4 3.3 copy-start.17
  222.5 150.6 %copy-start.1 = (f32[32,128,128]{2,1,0:T(8,128)S(1)}, f32[32,128,128]{2,1,0:T(8,128)}, u32[]{:S(2)}) copy-start(f32[32,128,128]{2,1,0:T(8,128)} %param.17) | copy-start | bytes 6291460
Sparse Core Ops, SparseCore 0:
  229.7 141.9 all-reduce.6
where the time goes:
time: 385 us; the launch traced here: 380 us
  waiting for transfers between devices  190 us (49%)
  local copies, waits for them, and re-layouts  77.9 us (20%)
  other arithmetic  35.2 us (9%)
  starting transfers between devices  32.5 us (8%)
  blocking collectives  22.2 us (6%)
  between operations  14.8 us (4%)
  matrix products  7.36 us (2%)
    unnamed x2, waiting for transfers between devices  139 us
    unnamed x49, local copies, waits for them, and re-layouts  28.7 us
    all_to_all x1, blocking collectives, to_columns(): lax.all_to_all(slab, 'lev', split_axis=2, concat_axis=0, tiled=True)  22.2 us
    all_to_all x1, waiting for transfers between devices, to_columns(): lax.all_to_all(lax.all_to_all(slab, 'lev', split_axis=2, concat_axis=0, t...  15.6 us
    all_to_all x1, waiting for transfers between devices, to_slabs(): lax.all_to_all(flipped, 'lev', split_axis=0, concat_axis=2, tiled=True)  15 us
    all_to_all x1, waiting for transfers between devices, to_slabs(): lax.all_to_all(lax.all_to_all(flipped, 'lev', split_axis=0, concat_axis=2...  14.4 us
    scatter-add x1, other arithmetic, local(): seed_field = jnp.zeros((final_field.size,), jnp.float32).at[receptor_cell...  12.3 us
    gather x1, local copies, waits for them, and re-layouts, local(): picked = final_field.reshape(-1)[receptor_cell]  11.8 us
  transfers between devices with their start and end apart: 8, of which 8 were waited for; matrix products, arithmetic and copies ran while one was open for 2% of the time, Pallas kernels for 0%

commit v1 on v0

v1 whole, which is shorter than its diff:
```python
import functools

import jax
import jax.numpy as jnp
from jax import lax
from jax.experimental import pallas as pl
from jax.experimental.pallas import tpu as pltpu
from jax.sharding import PartitionSpec as P

F32 = jnp.float32
BF16 = jnp.bfloat16
I32 = jnp.int32
MESH = pl.DeviceIdType.MESH
N_LEV = 8
N_ROW = 16
N = N_LEV * N_ROW
ROWS = 2048
REC_TILE = 512


def place(d):
    return (d // N_ROW, lax.rem(d, N_ROW))


def iota(shape, dim):
    return lax.broadcasted_iota(I32, shape, dim)


def swap4(v, unit):
    lane = iota(v[0].shape, 1)
    for bit in (1, 2):
        step = unit * bit
        high = (lane & step) != 0
        out = list(v)
        for a in range(4):
            if a & bit:
                continue
            b = a | bit
            out[a] = jnp.where(high, pltpu.roll(v[b], step, 1), v[a])
            out[b] = jnp.where(high, v[b], pltpu.roll(v[a], 128 - step, 1))
        v = out
    return v


def as_column(row):
    return jnp.broadcast_to(row, (128, 128)).T


def as_row(column):
    eye = iota((128, 128), 0) == iota((128, 128), 1)
    return jnp.sum(jnp.where(eye, jnp.broadcast_to(column, (128, 128)), 0.0), axis=0, keepdims=True)


def halves(v):
    high = v.astype(BF16)
    return high, (v - high.astype(F32)).astype(BF16)


def dot(a, b, dims):
    return lax.dot_general(a, b, (dims, ((), ())), preferred_element_type=F32)


def dot3(a, b, dims):
    ah, al = halves(a)
    bh, bl = halves(b)
    return dot(ah, bh, dims) + (dot(ah, bl, dims) + dot(al, bh, dims))


def one_hot(mask):
    return jnp.where(mask, 1.0, 0.0).astype(BF16)


def kernel(
    t_in, cx_in, cy_in, sx_in, sy_in, mat_in, rcell, rlim, scell, sdest, sslot, swt,
    final_out, cross_out, adj_out, inv_out,
    t, cx, cy, sx, sy, mat, work, cols, field, parts, hot, values, send_a, recv_a, recv_b, send_c, recv_c,
    halo_send, halo_recv, hback_send, hback_recv, picked,
    load_sem, own_sem, out_sem, hs_sem, hr_sem, as_sem, ar_sem, bs_sem, br_sem, cs_sem, cr_sem,
):
    my_lev = lax.axis_index("lev")
    my_row = lax.axis_index("row")
    me = my_lev * N_ROW + my_row
    up_row = lax.rem(my_row + 1, N_ROW)
    down_row = lax.rem(my_row + N_ROW - 1, N_ROW)

    loads = []
    for n, (src, dst) in enumerate(((t_in, t), (cx_in, cx), (cy_in, cy), (sx_in, sx), (sy_in, sy), (mat_in, mat))):
        c = pltpu.make_async_copy(src, dst, load_sem.at[n])
        c.start()
        loads.append(c)

    barrier = pltpu.get_barrier_semaphore()

    @pl.loop(1, N)
    def _(k):
        pl.semaphore_signal(barrier, inc=1, device_id=place(lax.rem(me + k, N)), device_id_type=MESH)

    loads[0].wait()
    halo_send[0] = t[pl.ds(3, 512, stride=4), :]
    halo_send[1] = t[pl.ds(0, 512, stride=4), :]
    pl.semaphore_wait(barrier, N - 1)

    def exchange(send, recv, rows, slot):
        c = pltpu.make_async_remote_copy(
            send.at[slot], recv.at[slot], hs_sem.at[rows + slot], hr_sem.at[rows + slot],
            device_id=(my_lev, (up_row, down_row)[slot]), device_id_type=MESH,
        )
        c.start()
        return c

    halo = [exchange(halo_send, halo_recv, 0, s) for s in (0, 1)]
    for c in loads[1:5]:
        c.wait()

    tile_row = iota((128, 128), 0)
    tile_lane = iota((128, 128), 1)
    strip_row = tile_row & 3

    def from_left(v):
        rolled = pltpu.roll(v, 1, 1)
        carried = jnp.where(tile_row < 4, 0.0, pltpu.roll(rolled, 4, 0))
        return jnp.where(tile_lane == 0, carried, rolled)

    def from_right(v):
        rolled = pltpu.roll(v, 127, 1)
        carried = jnp.where(tile_row >= 124, 0.0, pltpu.roll(rolled, 124, 0))
        return jnp.where(tile_lane == 127, carried, rolled)

    def from_before(v):
        return jnp.where(strip_row == 0, 0.0, pltpu.roll(v, 1, 0))

    def from_after(v):
        return jnp.where(strip_row == 3, 0.0, pltpu.roll(v, 127, 0))

    @pl.loop(0, 16)
    def _(lev):
        at = pl.ds(pl.multiple_of(lev * 128, 128), 128)
        v, a, b = t[at], cx[at], cy[at]
        work[at] = (
            (1.0 - a - b) * v
            + a * jnp.where(sx[at] != 0, from_before(v), from_after(v))
            + b * jnp.where(sy[at] != 0, from_left(v), from_right(v))
        )

    first = pl.ds(0, 512, stride=4)
    final = pl.ds(3, 512, stride=4)
    for c in halo:
        c.wait()
    has_down = jnp.where(my_row > 0, 1.0, 0.0)
    has_up = jnp.where(my_row < N_ROW - 1, 1.0, 0.0)
    work[first, :] = work[first, :] + has_down * jnp.where(sx[first, :] != 0, cx[first, :] * halo_recv[0], 0.0)
    work[final, :] = work[final, :] + has_up * jnp.where(sx[final, :] != 0, 0.0, cx[final, :] * halo_recv[1])

    low = iota((8, 128), 0) < 4
    here = my_row * N_LEV + my_lev

    @pl.loop(0, 16)
    def _(k):
        pair = lax.rem(k + me // 8, 16)
        at = pl.multiple_of(pair * 8, 8)
        groups = []
        for group in range(4):
            v = [work[pl.ds(pl.multiple_of((group * 4 + g) * 128 + at, 8), 8), :] for g in range(4)]
            groups.append(swap4(v, 32))
        for half in range(2):
            for q in range(4):
                a, b = groups[half * 2][q], groups[half * 2 + 1][q]
                send_a[at + q, half * 8:half * 8 + 8] = jnp.where(low, a, pltpu.roll(b, 4, 0))
                send_a[at + 4 + q, half * 8:half * 8 + 8] = jnp.where(low, pltpu.roll(a, 4, 0), b)

        @pl.loop(0, 8)
        def _(e):
            @pl.when(k + e > 0)
            def _():
                other = at + lax.rem(e + me, 8)
                pltpu.make_async_remote_copy(
                    send_a.at[other], recv_a.at[here], as_sem, ar_sem, device_id=place(other), device_id_type=MESH
                ).start()

            @pl.when(k + e == 0)
            def _():
                pltpu.make_async_copy(send_a.at[me], recv_a.at[here], own_sem).start()

    def all_of(send, recv, ss, rs):
        return pltpu.make_async_remote_copy(
            send.at[pl.ds(0, N - 1)], recv.at[pl.ds(0, N - 1)], ss, rs,
            device_id=(my_lev, up_row), device_id_type=MESH,
        )

    loads[5].wait()
    pltpu.make_async_copy(send_a.at[me], recv_a.at[here], own_sem).wait()
    flow = all_of(send_a, recv_a, as_sem, ar_sem)
    flow.wait_recv()

    @pl.loop(0, 16)
    def _(j):
        v = recv_a[pl.ds(j * 8, 8)].reshape(128, 128).T
        for r, u in enumerate(swap4([v[g * 32:g * 32 + 32] for g in range(4)], 1)):
            cols[pl.ds(pl.multiple_of(j * 128 + r * 32, 32), 32), :] = u

    @pl.loop(0, 32)
    def _(y):
        v = dot3(cols[pl.ds(y, 64, stride=32), :], mat[y], ((1,), (1,)))
        at = pl.ds(pl.multiple_of(y * 64, 64), 64)
        field[at] = v
        h, l = halves(v)
        parts[at, 0:128] = h
        parts[at, 128:256] = l

    final_copy = pltpu.make_async_copy(field, final_out, out_sem.at[0])
    final_copy.start()

    lanes = iota((REC_TILE, 128), 1)

    def column(ref, base):
        return jnp.concatenate([as_column(ref(base + s)) for s in range(REC_TILE // 128)], axis=0)

    def pick(base, row_of, lane_of, out):
        rows = column(row_of, base)
        for k in range(16):
            hot[:, k * 128:k * 128 + 128] = one_hot(rows == lanes + k * 128)
        g = dot(hot[...], parts[...], ((1,), (0,)))
        g = g[:, :128] + g[:, 128:]
        g = jnp.sum(jnp.where(column(lane_of, base) == lanes, g, 0.0), axis=1, keepdims=True)
        for s in range(REC_TILE // 128):
            out[pl.ds(base + s, 1), :] = as_row(g[s * 128:s * 128 + 128])

    @pl.loop(0, 4)
    def _(u):
        pick(u * 4, lambda s: rcell[pl.ds(s, 1), :] >> 7, lambda s: rcell[pl.ds(s, 1), :] & 127, picked)

    crossing = jax.nn.sigmoid(2.0 * (picked[...] - rlim[...]))
    cross_out[...] = crossing
    picked[...] = 2.0 * crossing * (1.0 - crossing)

    @pl.loop(0, 16)
    def _(u):
        seeds = as_column(picked[pl.ds(u, 1), :])
        mask = as_column(rcell[pl.ds(u, 1), :] & 127) == tile_lane
        h, l = halves(jnp.where(mask, seeds, 0.0))
        at = pl.ds(pl.multiple_of(u * 128, 128), 128)
        values[at, 0:128] = h
        values[at, 128:256] = l

    @pl.loop(0, 4)
    def _(u):
        rows = iota((REC_TILE, 128), 0) + u * REC_TILE
        for k in range(16):
            hot[:, k * 128:k * 128 + 128] = one_hot((rcell[k:k + 1, :] >> 7) == rows)
        g = dot(hot[...], values[...], ((1,), (0,)))
        work[pl.ds(pl.multiple_of(u * REC_TILE, REC_TILE), REC_TILE), :] = g[:, :128] + g[:, 128:]

    @pl.loop(0, 32)
    def _(y):
        at = pl.ds(pl.multiple_of(y * 64, 64), 64)
        cols[pl.ds(y, 64, stride=32), :] = dot3(work[at], mat[y], ((1,), (0,)))

    flow.wait_send()

    @pl.loop(0, 16)
    def _(k):
        j = lax.rem(k + my_row, N_ROW)
        v = [cols[pl.ds(pl.multiple_of(j * 128 + r * 32, 32), 32), :] for r in range(4)]
        v = jnp.concatenate(swap4(v, 1), axis=0).T
        send_a[pl.ds(j * 8, 8)] = v.reshape(8, 16, 128)

        @pl.loop(0, 8)
        def _(e):
            i = lax.rem(e + my_lev, N_LEV)

            @pl.when(k + e > 0)
            def _():
                pltpu.make_async_remote_copy(
                    send_a.at[j * 8 + i], recv_b.at[me], bs_sem, br_sem, device_id=(i, j), device_id_type=MESH
                ).start()

            @pl.when(k + e == 0)
            def _():
                pltpu.make_async_copy(send_a.at[here], recv_b.at[me], own_sem).start()

    pltpu.make_async_copy(send_a.at[here], recv_b.at[me], own_sem).wait()
    flow = all_of(send_a, recv_b, bs_sem, br_sem)
    flow.wait_recv()

    @pl.loop(0, 16)
    def _(pair):
        at = pl.multiple_of(pair * 8, 8)
        for half in range(2):
            va, vb = [], []
            for q in range(4):
                p = recv_b[at + q, half * 8:half * 8 + 8]
                s = recv_b[at + 4 + q, half * 8:half * 8 + 8]
                va.append(jnp.where(low, p, pltpu.roll(s, 4, 0)))
                vb.append(jnp.where(low, pltpu.roll(p, 4, 0), s))
            for group, v in ((half * 2, va), (half * 2 + 1, vb)):
                for g, u in enumerate(swap4(v, 32)):
                    t[pl.ds(pl.multiple_of((group * 4 + g) * 128 + at, 8), 8), :] = u

    hback_send[0] = jnp.where(sx[final, :] != 0, 0.0, cx[final, :] * t[final, :])
    hback_send[1] = jnp.where(sx[first, :] != 0, cx[first, :] * t[first, :], 0.0)
    halo = [exchange(hback_send, hback_recv, 2, s) for s in (0, 1)]

    @pl.loop(0, 16)
    def _(lev):
        at = pl.ds(pl.multiple_of(lev * 128, 128), 128)
        v, a, b = t[at], cx[at], cy[at]
        flux_x, flux_y = a * v, b * v
        lower_x, lower_y = sx[at] != 0, sy[at] != 0
        work[at] = (
            (1.0 - a - b) * v
            + from_after(jnp.where(lower_x, flux_x, 0.0))
            + from_before(jnp.where(lower_x, 0.0, flux_x))
            + from_right(jnp.where(lower_y, flux_y, 0.0))
            + from_left(jnp.where(lower_y, 0.0, flux_y))
        )

    for c in halo:
        c.wait()
    work[first, :] = work[first, :] + has_down * hback_recv[0]
    work[final, :] = work[final, :] + has_up * hback_recv[1]
    adj_copy = pltpu.make_async_copy(work, adj_out, out_sem.at[1])
    adj_copy.start()

    @pl.loop(0, 16)
    def _(lev):
        at = pl.ds(pl.multiple_of(lev * 128, 128), 128)
        h, l = halves(work[at])
        parts[at, 0:128] = h
        parts[at, 128:256] = l

    def stack_row(s):
        c = scell[pl.ds(s, 1), :]
        return (c >> 14) * 128 + ((c >> 7) & 31) * 4 + ((c >> 12) & 3)

    pick(0, stack_row, lambda s: scell[pl.ds(s, 1), :] & 127, picked)
    stack_values = picked[0:4, :] * swt[...]
    partial = jnp.zeros((128, 256), F32)
    wide = iota((128, 256), 1)
    for s in range(4):
        owner = one_hot(sdest[s:s + 1, :] == tile_row)
        slot = as_column(sslot[s:s + 1, :])
        amount = as_column(stack_values[s:s + 1, :])
        slot = jnp.concatenate([slot, slot], axis=1)
        amount = jnp.concatenate([amount, amount], axis=1)
        h, l = halves(jnp.where(slot == wide, amount, 0.0))
        partial = partial + (dot(owner, h, ((1,), (0,))) + dot(owner, l, ((1,), (0,))))
    send_c[:, 0, :] = partial[:, :128]
    send_c[:, 1, :] = partial[:, 128:]

    @pl.loop(1, N)
    def _(k):
        other = lax.rem(me + k, N)
        pltpu.make_async_remote_copy(
            send_c.at[other], recv_c.at[me], cs_sem, cr_sem, device_id=place(other), device_id_type=MESH
        ).start()

    own = pltpu.make_async_copy(send_c.at[me], recv_c.at[me], own_sem)
    own.start()
    own.wait()
    last = all_of(send_c, recv_c, cs_sem, cr_sem)
    last.wait_recv()
    inv_out[...] = jnp.sum(recv_c[...], axis=0)
    last.wait_send()
    flow.wait_send()
    final_copy.wait()
    adj_copy.wait()


def rows_of(slab):
    return slab.reshape(16, 4, 32, 128).transpose(0, 2, 1, 3).reshape(ROWS, 128)


def local(
    tracer, courant_x, courant_y, wind_x, wind_y, inverse_diffusion,
    receptor_cell, receptor_limit, stack_cell, stack_dest, stack_slot, stack_weight,
):
    vmem = pl.BlockSpec(memory_space=pltpu.VMEM)
    hbm = pl.BlockSpec(memory_space=pl.ANY)
    slab = pltpu.VMEM((ROWS, 128), F32)
    dma = pltpu.SemaphoreType.DMA
    blocks = pltpu.VMEM((N, 16, 128), F32)
    edge = pltpu.VMEM((2, 512, 128), F32)
    final_field, crossing, adjoint, inventory = pl.pallas_call(
        kernel,
        out_shape=(
            jax.ShapeDtypeStruct((ROWS, 128), F32),
            jax.ShapeDtypeStruct((16, 128), F32),
            jax.ShapeDtypeStruct((ROWS, 128), F32),
            jax.ShapeDtypeStruct((2, 128), F32),
        ),
        in_specs=[hbm] * 6 + [vmem] * 6,
        out_specs=(hbm, vmem, hbm, vmem),
        scratch_shapes=[
            slab, slab, slab, pltpu.VMEM((ROWS, 128), I32), pltpu.VMEM((ROWS, 128), I32), pltpu.VMEM((32, 128, 128), F32),
            slab, slab, slab, pltpu.VMEM((ROWS, 256), BF16), pltpu.VMEM((REC_TILE, ROWS), BF16),
            pltpu.VMEM((ROWS, 256), BF16), blocks, blocks, blocks,
            pltpu.VMEM((N, 2, 128), F32), pltpu.VMEM((N, 2, 128), F32),
            edge, edge, edge, edge, pltpu.VMEM((16, 128), F32),
            dma((6,)), dma, dma((2,)), dma((4,)), dma((4,)), dma, dma, dma, dma, dma, dma,
        ],
        compiler_params=pltpu.CompilerParams(
            collective_id=0, has_side_effects=True, vmem_limit_bytes=56 * 1024 * 1024
        ),
        name="transport",
    )(
        rows_of(tracer), rows_of(courant_x), rows_of(courant_y), rows_of(wind_x), rows_of(wind_y), inverse_diffusion,
        receptor_cell.reshape(16, 128), receptor_limit.reshape(16, 128), stack_cell.reshape(4, 128),
        stack_dest.reshape(4, 128), stack_slot.reshape(4, 128), stack_weight.reshape(4, 128),
    )
    adjoint = adjoint.reshape(16, 32, 4, 128).transpose(0, 2, 1, 3).reshape(16, 4, 4096)
    return final_field.reshape(32, 64, 128), crossing.reshape(-1), adjoint, inventory.reshape(-1)


def solution(mesh):
    slab = P("lev", "row", None)
    flat = P(("lev", "row"))
    return jax.shard_map(
        local,
        mesh=mesh,
        in_specs=(slab,) * 5 + (P(("lev", "row"), None, None), flat, flat, flat, P(("lev", "row"), None), flat, flat),
        out_specs=(P(("lev", "row"), None, None), flat, slab, flat),
        check_vma=False,
    )
```

time: 385 us -> 108 us (0.28); the launches traced: 380 us -> 108 us
  waiting for transfers between devices: 190 us -> 0 us
  Pallas kernels: 0 us -> 102 us
  local copies, waits for them, and re-layouts: 77.9 us -> 4.54 us
  other arithmetic: 35.2 us -> 0 us
  starting transfers between devices: 32.5 us -> 0 us
  blocking collectives: 22.2 us -> 0 us
  between operations: 14.8 us -> 0.67 us
  matrix products: 7.36 us -> 0 us
    unnamed x2 -> x0, waiting for transfers between devices: 139 us -> none
    pallas_call x0 -> x1, Pallas kernels: none -> 102 us  [local(): pl.pallas_call(kernel, out_shape=(jax.ShapeDtypeStruct((ROWS, 128), F32),...]
    all_to_all x3 -> x0, waiting for transfers between devices: 45 us -> none  [the longest x1 15.6 us: to_columns(): lax.all_to_all(lax.all_to_all(slab, 'lev', split_axis=2, concat_axis=0, t...]
    unnamed x49 -> x10, local copies, waits for them, and re-layouts: 28.7 us -> 4.54 us
    all_to_all x1 -> x0, blocking collectives: 22.2 us -> none  [to_columns(): lax.all_to_all(slab, 'lev', split_axis=2, concat_axis=0, tiled=True)]
    all_to_all x3 -> x0, starting transfers between devices: 20.7 us -> none  [the longest x1 10.5 us: to_columns(): lax.all_to_all(lax.all_to_all(slab, 'lev', split_axis=2, concat_axis=0, t...]
    scatter-add x2 -> x0, other arithmetic: 16.1 us -> none  [the longest x1 12.3 us: local(): seed_field = jnp.zeros((final_field.size,), jnp.float32).at[receptor_cell...]
    gather x2 -> x0, local copies, waits for them, and re-layouts: 14.9 us -> none  [the longest x1 11.8 us: local(): picked = final_field.reshape(-1)[receptor_cell]]
  transfers between devices with their start and end apart: 8 -> 0, of which waited for: 8 -> 0; matrix products, arithmetic and copies ran while one was open for 2% -> 0% of each run, Pallas kernels for 0% -> 0%
where the time goes in v1:
time: 108 us
  Pallas kernels  102 us (94%)
  local copies, waits for them, and re-layouts  4.54 us (4%)
    pallas_call x1, Pallas kernels, local(): pl.pallas_call(kernel, out_shape=(jax.ShapeDtypeStruct((ROWS, 128), F32),...  102 us
    unnamed x10, local copies, waits for them, and re-layouts  4.54 us

profile of v1, /device:TPU:1, one launch (start us, length us, event | category | flops | bytes accessed | tf_op | source)
XLA Modules:
  0.0 107.6 jit_solution(18022256446008207963)
XLA Ops:
  0.6 102.4 %transport.1 = (f32[2048,128]{1,0:T(8,128)}, f32[16,128]{1,0:T(8,128)}, f32[2048,128]{1,0:T(8,128)}, f32[2,128]{1,0:T(2,128)}) custom-call(f32[2048,128]{1,0:T(8,128)} %bitcast.41, f32[2048,128]{1,0:T(8,128)} %bitcast.42, f32[2048,128]{1,0:T(8,128)} %bitcast.43, s32[2048,128]{1,0:T(8,128)} %bitcast.44, s32[2048,128]{1,0:T(8,128)} %bitcast.45, ...), custom_call_target="tpu_custom_call" | custom-call | tf_op jit(solution)/shard_map/transport/pallas_call | solution.py:383
  103.1 0.0 copy-start.1
  103.1 0.0 copy-start
  103.1 0.0 copy-start.2
  103.1 2.4 %copy.26 = f32[32,64,128]{2,1,0:T(8,128)} copy(f32[32,64,128]{2,1,0:T(8,128)} %bitcast.40) | data formatting | bytes 2097152
  105.5 0.0 copy-done.1
  105.5 0.6 copy.27
  106.1 0.0 copy-done
  106.1 1.0 copy.28
  107.1 0.0 copy-done.2
  107.1 0.6 copy.29
Async XLA Ops:
  103.1 2.4 %copy-start.1 = (f32[16,128]{1,0:T(8,128)S(1)}, f32[16,128]{1,0:T(8,128)}, u32[]{:S(2)}) copy-start(f32[16,128]{1,0:T(8,128)} %get-tuple-element.9) | copy-start | bytes 24580
  103.1 3.0 %copy-start = (f32[2048,128]{1,0:T(8,128)S(1)}, f32[2048,128]{1,0:T(8,128)}, u32[]{:S(2)}) copy-start(f32[2048,128]{1,0:T(8,128)} %get-tuple-element.10) | copy-start | bytes 3145732
  103.1 4.0 %copy-start.2 = (f32[2,128]{1,0:T(2,128)S(1)}, f32[2,128]{1,0:T(2,128)}, u32[]{:S(2)}) copy-start(f32[2,128]{1,0:T(2,128)} %get-tuple-element.11) | copy-start | bytes 3076

commit v2 on v1

--- a/solution.py
+++ b/solution.py
@@ -60,10 +60,11 @@
     return lax.dot_general(a, b, (dims, ((), ())), preferred_element_type=F32)
 
 
-def dot3(a, b, dims):
-    ah, al = halves(a)
-    bh, bl = halves(b)
-    return dot(ah, bh, dims) + (dot(ah, bl, dims) + dot(al, bh, dims))
+def dot_split(a, b, dims):
+    n = a.shape[0]
+    side = 0 if dims[1] == (1,) else 1
+    g = dot(jnp.concatenate(halves(a), axis=0), jnp.concatenate(halves(b), axis=side), dims)
+    return (g[:n, :128] + g[n:, :128]) + (g[:n, 128:] + g[n:, 128:])
 
 
 def one_hot(mask):
@@ -73,9 +74,9 @@
 def kernel(
     t_in, cx_in, cy_in, sx_in, sy_in, mat_in, rcell, rlim, scell, sdest, sslot, swt,
     final_out, cross_out, adj_out, inv_out,
-    t, cx, cy, sx, sy, mat, work, cols, field, parts, hot, values, send_a, recv_a, recv_b, send_c, recv_c,
+    t, cx, cy, sx, sy, mat, work, cols, field, parts, hot, values, send_a, recv_a, recv_b, level_send, level_recv, row_send, row_recv,
     halo_send, halo_recv, hback_send, hback_recv, picked,
-    load_sem, own_sem, out_sem, hs_sem, hr_sem, as_sem, ar_sem, bs_sem, br_sem, cs_sem, cr_sem,
+    load_sem, own_sem, out_sem, hs_sem, hr_sem, as_sem, ar_sem, bs_sem, br_sem, cs_sem, cr_sem, ready,
 ):
     my_lev = lax.axis_index("lev")
     my_row = lax.axis_index("row")
@@ -91,14 +92,26 @@
 
     barrier = pltpu.get_barrier_semaphore()
 
-    @pl.loop(1, N)
-    def _(k):
-        pl.semaphore_signal(barrier, inc=1, device_id=place(lax.rem(me + k, N)), device_id_type=MESH)
+    @pl.loop(1, N_ROW)
+    def _(k):
+        other = (my_lev, lax.rem(my_row + k, N_ROW))
+        pl.semaphore_signal(barrier, inc=1, device_id=other, device_id_type=MESH)
+
+    @pl.loop(1, N_LEV)
+    def _(k):
+        other = (lax.rem(my_lev + k, N_LEV), my_row)
+        pl.semaphore_signal(barrier, inc=1, device_id=other, device_id_type=MESH)
 
     loads[0].wait()
     halo_send[0] = t[pl.ds(3, 512, stride=4), :]
     halo_send[1] = t[pl.ds(0, 512, stride=4), :]
-    pl.semaphore_wait(barrier, N - 1)
+    pl.semaphore_wait(barrier, N_ROW + N_LEV - 2)
+
+    @pl.loop(1, N_ROW)
+    def _(k):
+        other = (my_lev, lax.rem(my_row + k, N_ROW))
+        pl.semaphore_signal(ready, inc=1, device_id=other, device_id_type=MESH)
+
 
     def exchange(send, recv, rows, slot):
         c = pltpu.make_async_remote_copy(
@@ -150,6 +163,8 @@
     has_up = jnp.where(my_row < N_ROW - 1, 1.0, 0.0)
     work[first, :] = work[first, :] + has_down * jnp.where(sx[first, :] != 0, cx[first, :] * halo_recv[0], 0.0)
     work[final, :] = work[final, :] + has_up * jnp.where(sx[final, :] != 0, 0.0, cx[final, :] * halo_recv[1])
+
+    pl.semaphore_wait(ready, N_ROW - 1)
 
     low = iota((8, 128), 0) < 4
     here = my_row * N_LEV + my_lev
@@ -192,15 +207,15 @@
     flow = all_of(send_a, recv_a, as_sem, ar_sem)
     flow.wait_recv()
 
-    @pl.loop(0, 16)
+    @pl.loop(0, 16, unroll=2)
     def _(j):
         v = recv_a[pl.ds(j * 8, 8)].reshape(128, 128).T
         for r, u in enumerate(swap4([v[g * 32:g * 32 + 32] for g in range(4)], 1)):
             cols[pl.ds(pl.multiple_of(j * 128 + r * 32, 32), 32), :] = u
 
-    @pl.loop(0, 32)
+    @pl.loop(0, 32, unroll=4)
     def _(y):
-        v = dot3(cols[pl.ds(y, 64, stride=32), :], mat[y], ((1,), (1,)))
+        v = dot_split(cols[pl.ds(y, 64, stride=32), :], mat[y], ((1,), (1,)))
         at = pl.ds(pl.multiple_of(y * 64, 64), 64)
         field[at] = v
         h, l = halves(v)
@@ -250,10 +265,10 @@
         g = dot(hot[...], values[...], ((1,), (0,)))
         work[pl.ds(pl.multiple_of(u * REC_TILE, REC_TILE), REC_TILE), :] = g[:, :128] + g[:, 128:]
 
-    @pl.loop(0, 32)
+    @pl.loop(0, 32, unroll=4)
     def _(y):
         at = pl.ds(pl.multiple_of(y * 64, 64), 64)
-        cols[pl.ds(y, 64, stride=32), :] = dot3(work[at], mat[y], ((1,), (0,)))
+        cols[pl.ds(y, 64, stride=32), :] = dot_split(work[at], mat[y], ((1,), (0,)))
 
     flow.wait_send()
 
@@ -344,26 +359,61 @@
         amount = jnp.concatenate([amount, amount], axis=1)
         h, l = halves(jnp.where(slot == wide, amount, 0.0))
         partial = partial + (dot(owner, h, ((1,), (0,))) + dot(owner, l, ((1,), (0,))))
-    send_c[:, 0, :] = partial[:, :128]
-    send_c[:, 1, :] = partial[:, 128:]
-
-    @pl.loop(1, N)
-    def _(k):
-        other = lax.rem(me + k, N)
+    level_send[...] = partial.reshape(N_LEV, N_ROW, 256)
+    level_recv[my_lev] = level_send[my_lev]
+
+    @pl.loop(1, N_LEV)
+    def _(k):
+        other = lax.rem(my_lev + k, N_LEV)
         pltpu.make_async_remote_copy(
-            send_c.at[other], recv_c.at[me], cs_sem, cr_sem, device_id=place(other), device_id_type=MESH
+            level_send.at[other], level_recv.at[my_lev], cs_sem.at[0], cr_sem.at[0],
+            device_id=(other, my_row), device_id_type=MESH,
         ).start()
 
-    own = pltpu.make_async_copy(send_c.at[me], recv_c.at[me], own_sem)
-    own.start()
-    own.wait()
-    last = all_of(send_c, recv_c, cs_sem, cr_sem)
+    def all_but_one(send, recv, n, slot):
+        return pltpu.make_async_remote_copy(
+            send.at[pl.ds(0, n - 1)], recv.at[pl.ds(0, n - 1)], cs_sem.at[slot], cr_sem.at[slot],
+            device_id=(my_lev, up_row), device_id_type=MESH,
+        )
+
+    levels = all_but_one(level_send, level_recv, N_LEV, 0)
+    levels.wait_recv()
+    total = jnp.sum(level_recv[...], axis=0)
+    row_send[:, 0, :] = total[:, :128]
+    row_send[:, 1, :] = total[:, 128:]
+    row_recv[my_row] = row_send[my_row]
+
+    @pl.loop(1, N_ROW)
+    def _(k):
+        other = lax.rem(my_row + k, N_ROW)
+        pltpu.make_async_remote_copy(
+            row_send.at[other], row_recv.at[my_row], cs_sem.at[1], cr_sem.at[1],
+            device_id=(my_lev, other), device_id_type=MESH,
+        ).start()
+
+    last = all_but_one(row_send, row_recv, N_ROW, 1)
     last.wait_recv()
-    inv_out[...] = jnp.sum(recv_c[...], axis=0)
+    inv_out[...] = jnp.sum(row_recv[...], axis=0)
+    levels.wait_send()
     last.wait_send()
     flow.wait_send()
     final_copy.wait()
     adj_copy.wait()
+
+
+def write_out(*refs):
+    n = len(refs) // 2
+    sems = refs[-1]
+    copies = []
+    for a, b in zip(refs[:n], refs[n:-1]):
+        rows = a.shape[0]
+        step = min(rows, 512)
+        for at in range(0, rows, step):
+            c = pltpu.make_async_copy(a.at[pl.ds(at, step)], b.at[pl.ds(at, step)], sems.at[len(copies)])
+            c.start()
+            copies.append(c)
+    for c in copies:
+        c.wait()
 
 
 def rows_of(slab):
@@ -380,7 +430,7 @@
     dma = pltpu.SemaphoreType.DMA
     blocks = pltpu.VMEM((N, 16, 128), F32)
     edge = pltpu.VMEM((2, 512, 128), F32)
-    final_field, crossing, adjoint, inventory = pl.pallas_call(
+    results = pl.pallas_call(
         kernel,
         out_shape=(
             jax.ShapeDtypeStruct((ROWS, 128), F32),
@@ -394,9 +444,10 @@
             slab, slab, slab, pltpu.VMEM((ROWS, 128), I32), pltpu.VMEM((ROWS, 128), I32), pltpu.VMEM((32, 128, 128), F32),
             slab, slab, slab, pltpu.VMEM((ROWS, 256), BF16), pltpu.VMEM((REC_TILE, ROWS), BF16),
             pltpu.VMEM((ROWS, 256), BF16), blocks, blocks, blocks,
-            pltpu.VMEM((N, 2, 128), F32), pltpu.VMEM((N, 2, 128), F32),
+            pltpu.VMEM((N_LEV, N_ROW, 256), F32), pltpu.VMEM((N_LEV, N_ROW, 256), F32),
+            pltpu.VMEM((N_ROW, 2, 128), F32), pltpu.VMEM((N_ROW, 2, 128), F32),
             edge, edge, edge, edge, pltpu.VMEM((16, 128), F32),
-            dma((6,)), dma, dma((2,)), dma((4,)), dma((4,)), dma, dma, dma, dma, dma, dma,
+            dma((6,)), dma, dma((2,)), dma((4,)), dma((4,)), dma, dma, dma, dma, dma((2,)), dma((2,)), pltpu.SemaphoreType.REGULAR,
         ],
         compiler_params=pltpu.CompilerParams(
             collective_id=0, has_side_effects=True, vmem_limit_bytes=56 * 1024 * 1024
@@ -407,6 +458,14 @@
         receptor_cell.reshape(16, 128), receptor_limit.reshape(16, 128), stack_cell.reshape(4, 128),
         stack_dest.reshape(4, 128), stack_slot.reshape(4, 128), stack_weight.reshape(4, 128),
     )
+    final_field, crossing, adjoint, inventory = pl.pallas_call(
+        write_out,
+        out_shape=tuple(jax.ShapeDtypeStruct(r.shape, r.dtype) for r in results),
+        in_specs=[hbm] * 4,
+        out_specs=(hbm,) * 4,
+        scratch_shapes=[dma((10,))],
+        name="write_out",
+    )(*results)
     adjoint = adjoint.reshape(16, 32, 4, 128).transpose(0, 2, 1, 3).reshape(16, 4, 4096)
     return final_field.reshape(32, 64, 128), crossing.reshape(-1), adjoint, inventory.reshape(-1)
 

time: 108 us -> 155 us (1.44)
  Pallas kernels: 102 us -> 154 us
  local copies, waits for them, and re-layouts: 4.54 us -> 0 us
    pallas_call x0 -> x1, Pallas kernels: none -> 65 us  [local(): pl.pallas_call(write_out, out_shape=tuple((jax.ShapeDtypeStruct(r.shape,...]
    pallas_call x1, Pallas kernels: 102 us -> 89.1 us  [local(): pl.pallas_call(kernel, out_shape=(jax.ShapeDtypeStruct((ROWS, 128), F32),...]
    unnamed x10 -> x0, local copies, waits for them, and re-layouts: 4.54 us -> none
where the time goes in v2:
time: 155 us
  Pallas kernels  154 us (99%)
    pallas_call x1, Pallas kernels, local(): pl.pallas_call(kernel, out_shape=(jax.ShapeDtypeStruct((ROWS, 128), F32),...  89.1 us
    pallas_call x1, Pallas kernels, local(): pl.pallas_call(write_out, out_shape=tuple((jax.ShapeDtypeStruct(r.shape,...  65 us

profile of v2, /device:TPU:1, one launch (start us, length us, event | category | flops | bytes accessed | tf_op | source)
XLA Modules:
  0.0 154.7 jit_solution(1722632974405739258)
XLA Ops:
  0.6 89.1 %transport.1 = (f32[2048,128]{1,0:T(8,128)}, f32[16,128]{1,0:T(8,128)}, f32[2048,128]{1,0:T(8,128)}, f32[2,128]{1,0:T(2,128)}) custom-call(f32[2048,128]{1,0:T(8,128)} %bitcast.39, f32[2048,128]{1,0:T(8,128)} %bitcast.40, f32[2048,128]{1,0:T(8,128)} %bitcast.41, s32[2048,128]{1,0:T(8,128)} %bitcast.42, s32[2048,128]{1,0:T(8,128)} %bitcast.43, ...), custom_call_target="tpu_custom_call" | custom-call | tf_op jit(solution)/shard_map/transport/pallas_call | solution.py:433
  89.7 65.0 %write_out.1 = (f32[2048,128]{1,0:T(8,128)}, f32[16,128]{1,0:T(8,128)}, f32[2048,128]{1,0:T(8,128)}, f32[2,128]{1,0:T(2,128)}) custom-call(f32[2048,128]{1,0:T(8,128)} %get-tuple-element.12.refs_0_, f32[16,128]{1,0:T(8,128)} %get-tuple-element.13.refs_1_, f32[2048,128]{1,0:T(8,128)} %get-tuple-element.14.refs_2_, f32[2,128]{1,0:T(2,128)} %get-tuple-element.15.refs_3_), custom_call_target="tpu_custom_call" | custom-call | tf_op jit(solution)/shard_map/write_out/pallas_call | solution.py:461

commit v3 on v2

--- a/solution.py
+++ b/solution.py
@@ -103,8 +103,11 @@
         pl.semaphore_signal(barrier, inc=1, device_id=other, device_id_type=MESH)
 
     loads[0].wait()
-    halo_send[0] = t[pl.ds(3, 512, stride=4), :]
-    halo_send[1] = t[pl.ds(0, 512, stride=4), :]
+    my_y = my_lev // 2
+    for slot, start in ((0, 3), (1, 0)):
+        edge = t[pl.ds(start, 512, stride=4), :].reshape(16, 4, 8, 128)
+        for p in range(4):
+            halo_send[slot, p] = edge[:, p].reshape(128, 128)
     pl.semaphore_wait(barrier, N_ROW + N_LEV - 2)
 
     @pl.loop(1, N_ROW)
@@ -113,15 +116,17 @@
         pl.semaphore_signal(ready, inc=1, device_id=other, device_id_type=MESH)
 
 
-    def exchange(send, recv, rows, slot):
-        c = pltpu.make_async_remote_copy(
-            send.at[slot], recv.at[slot], hs_sem.at[rows + slot], hr_sem.at[rows + slot],
+    def exchange(send, recv, base, slot, p):
+        return pltpu.make_async_remote_copy(
+            send.at[slot, p], recv.at[slot, p], hs_sem.at[base + slot, p], hr_sem.at[base + slot, p],
             device_id=(my_lev, (up_row, down_row)[slot]), device_id_type=MESH,
         )
-        c.start()
-        return c
-
-    halo = [exchange(halo_send, halo_recv, 0, s) for s in (0, 1)]
+
+    @pl.loop(0, 4)
+    def _(w):
+        for slot in range(2):
+            exchange(halo_send, halo_recv, 0, slot, lax.rem(my_y + w, 4)).start()
+
     for c in loads[1:5]:
         c.wait()
 
@@ -155,46 +160,56 @@
             + b * jnp.where(sy[at] != 0, from_left(v), from_right(v))
         )
 
-    first = pl.ds(0, 512, stride=4)
-    final = pl.ds(3, 512, stride=4)
-    for c in halo:
-        c.wait()
     has_down = jnp.where(my_row > 0, 1.0, 0.0)
     has_up = jnp.where(my_row < N_ROW - 1, 1.0, 0.0)
-    work[first, :] = work[first, :] + has_down * jnp.where(sx[first, :] != 0, cx[first, :] * halo_recv[0], 0.0)
-    work[final, :] = work[final, :] + has_up * jnp.where(sx[final, :] != 0, 0.0, cx[final, :] * halo_recv[1])
+
+    def edge_rows(lev, p, r):
+        return pl.ds(lev * 128 + p * 32 + r, 8, stride=4)
 
     pl.semaphore_wait(ready, N_ROW - 1)
 
     low = iota((8, 128), 0) < 4
     here = my_row * N_LEV + my_lev
 
-    @pl.loop(0, 16)
-    def _(k):
-        pair = lax.rem(k + me // 8, 16)
-        at = pl.multiple_of(pair * 8, 8)
-        groups = []
-        for group in range(4):
-            v = [work[pl.ds(pl.multiple_of((group * 4 + g) * 128 + at, 8), 8), :] for g in range(4)]
-            groups.append(swap4(v, 32))
-        for half in range(2):
-            for q in range(4):
-                a, b = groups[half * 2][q], groups[half * 2 + 1][q]
-                send_a[at + q, half * 8:half * 8 + 8] = jnp.where(low, a, pltpu.roll(b, 4, 0))
-                send_a[at + 4 + q, half * 8:half * 8 + 8] = jnp.where(low, pltpu.roll(a, 4, 0), b)
-
-        @pl.loop(0, 8)
-        def _(e):
-            @pl.when(k + e > 0)
-            def _():
-                other = at + lax.rem(e + me, 8)
-                pltpu.make_async_remote_copy(
-                    send_a.at[other], recv_a.at[here], as_sem, ar_sem, device_id=place(other), device_id_type=MESH
-                ).start()
-
-            @pl.when(k + e == 0)
-            def _():
-                pltpu.make_async_copy(send_a.at[me], recv_a.at[here], own_sem).start()
+    @pl.loop(0, 4)
+    def _(w):
+        p = lax.rem(my_y + w, 4)
+        for slot in range(2):
+            exchange(halo_send, halo_recv, 0, slot, p).wait()
+        for lev in range(16):
+            e = edge_rows(lev, p, 0)
+            v = cx[e, :] * halo_recv[0, p, lev * 8:lev * 8 + 8]
+            work[e, :] = work[e, :] + has_down * jnp.where(sx[e, :] != 0, v, 0.0)
+            e = edge_rows(lev, p, 3)
+            v = cx[e, :] * halo_recv[1, p, lev * 8:lev * 8 + 8]
+            work[e, :] = work[e, :] + has_up * jnp.where(sx[e, :] != 0, 0.0, v)
+
+        @pl.loop(0, 4)
+        def _(k):
+            pair = p * 4 + lax.rem(k + me // 8, 4)
+            at = pl.multiple_of(pair * 8, 8)
+            groups = []
+            for group in range(4):
+                v = [work[pl.ds(pl.multiple_of((group * 4 + g) * 128 + at, 8), 8), :] for g in range(4)]
+                groups.append(swap4(v, 32))
+            for half in range(2):
+                for q in range(4):
+                    a, b = groups[half * 2][q], groups[half * 2 + 1][q]
+                    send_a[at + q, half * 8:half * 8 + 8] = jnp.where(low, a, pltpu.roll(b, 4, 0))
+                    send_a[at + 4 + q, half * 8:half * 8 + 8] = jnp.where(low, pltpu.roll(a, 4, 0), b)
+
+            @pl.loop(0, 8)
+            def _(e):
+                @pl.when(w + k + e > 0)
+                def _():
+                    other = at + lax.rem(e + me, 8)
+                    pltpu.make_async_remote_copy(
+                        send_a.at[other], recv_a.at[here], as_sem, ar_sem, device_id=place(other), device_id_type=MESH
+                    ).start()
+
+                @pl.when(w + k + e == 0)
+                def _():
+                    pltpu.make_async_copy(send_a.at[me], recv_a.at[here], own_sem).start()
 
     def all_of(send, recv, ss, rs):
         return pltpu.make_async_remote_copy(
@@ -272,48 +287,70 @@
 
     flow.wait_send()
 
+    def send_back(w, j, core):
+        i = 2 * lax.rem(my_y + w, 4) + core
+        block = j * N_LEV + i
+        at_home = (i == my_lev) & (j == my_row)
+
+        @pl.when(jnp.logical_not(at_home))
+        def _():
+            pltpu.make_async_remote_copy(
+                send_a.at[block], recv_b.at[me], bs_sem.at[w], br_sem.at[w], device_id=(i, j), device_id_type=MESH
+            ).start()
+
+        @pl.when(at_home)
+        def _():
+            pltpu.make_async_copy(send_a.at[here], recv_b.at[me], own_sem).start()
+
     @pl.loop(0, 16)
     def _(k):
-        j = lax.rem(k + my_row, N_ROW)
+        j = lax.rem(5 * k + my_row, N_ROW)
         v = [cols[pl.ds(pl.multiple_of(j * 128 + r * 32, 32), 32), :] for r in range(4)]
         v = jnp.concatenate(swap4(v, 1), axis=0).T
         send_a[pl.ds(j * 8, 8)] = v.reshape(8, 16, 128)
 
-        @pl.loop(0, 8)
-        def _(e):
-            i = lax.rem(e + my_lev, N_LEV)
-
-            @pl.when(k + e > 0)
-            def _():
-                pltpu.make_async_remote_copy(
-                    send_a.at[j * 8 + i], recv_b.at[me], bs_sem, br_sem, device_id=(i, j), device_id_type=MESH
-                ).start()
-
-            @pl.when(k + e == 0)
-            def _():
-                pltpu.make_async_copy(send_a.at[here], recv_b.at[me], own_sem).start()
+        for core in range(2):
+            send_back(0, j, core)
+
+    @pl.loop(1, 4)
+    def _(w):
+        @pl.loop(0, 16)
+        def _(k):
+            for core in range(2):
+                send_back(w, lax.rem(5 * k + my_row, N_ROW), core)
+
+    def wave(w, n):
+        return pltpu.make_async_remote_copy(
+            send_a.at[pl.ds(0, n)], recv_b.at[pl.ds(0, n)], bs_sem.at[w], br_sem.at[w],
+            device_id=(my_lev, up_row), device_id_type=MESH,
+        )
 
     pltpu.make_async_copy(send_a.at[here], recv_b.at[me], own_sem).wait()
-    flow = all_of(send_a, recv_b, bs_sem, br_sem)
-    flow.wait_recv()
-
-    @pl.loop(0, 16)
-    def _(pair):
-        at = pl.multiple_of(pair * 8, 8)
-        for half in range(2):
-            va, vb = [], []
-            for q in range(4):
-                p = recv_b[at + q, half * 8:half * 8 + 8]
-                s = recv_b[at + 4 + q, half * 8:half * 8 + 8]
-                va.append(jnp.where(low, p, pltpu.roll(s, 4, 0)))
-                vb.append(jnp.where(low, pltpu.roll(p, 4, 0), s))
-            for group, v in ((half * 2, va), (half * 2 + 1, vb)):
-                for g, u in enumerate(swap4(v, 32)):
-                    t[pl.ds(pl.multiple_of((group * 4 + g) * 128 + at, 8), 8), :] = u
-
-    hback_send[0] = jnp.where(sx[final, :] != 0, 0.0, cx[final, :] * t[final, :])
-    hback_send[1] = jnp.where(sx[first, :] != 0, cx[first, :] * t[first, :], 0.0)
-    halo = [exchange(hback_send, hback_recv, 2, s) for s in (0, 1)]
+    for w in range(4):
+        wave(w, 31 if w == 0 else 32).wait_recv()
+        p = lax.rem(my_y + 4 - w, 4)
+
+        @pl.loop(0, 4)
+        def _(k):
+            at = pl.multiple_of((p * 4 + k) * 8, 8)
+            for half in range(2):
+                va, vb = [], []
+                for q in range(4):
+                    u = recv_b[at + q, half * 8:half * 8 + 8]
+                    s = recv_b[at + 4 + q, half * 8:half * 8 + 8]
+                    va.append(jnp.where(low, u, pltpu.roll(s, 4, 0)))
+                    vb.append(jnp.where(low, pltpu.roll(u, 4, 0), s))
+                for group, v in ((half * 2, va), (half * 2 + 1, vb)):
+                    for g, u in enumerate(swap4(v, 32)):
+                        t[pl.ds(pl.multiple_of((group * 4 + g) * 128 + at, 8), 8), :] = u
+
+        for lev in range(16):
+            e = edge_rows(lev, p, 3)
+            hback_send[0, p, lev * 8:lev * 8 + 8] = jnp.where(sx[e, :] != 0, 0.0, cx[e, :] * t[e, :])
+            e = edge_rows(lev, p, 0)
+            hback_send[1, p, lev * 8:lev * 8 + 8] = jnp.where(sx[e, :] != 0, cx[e, :] * t[e, :], 0.0)
+        for slot in range(2):
+            exchange(hback_send, hback_recv, 2, slot, p).start()
 
     @pl.loop(0, 16)
     def _(lev):
@@ -329,10 +366,19 @@
             + from_left(jnp.where(lower_y, 0.0, flux_y))
         )
 
-    for c in halo:
-        c.wait()
-    work[first, :] = work[first, :] + has_down * hback_recv[0]
-    work[final, :] = work[final, :] + has_up * hback_recv[1]
+    for p in range(4):
+        for slot in range(2):
+            exchange(hback_send, hback_recv, 2, slot, p).wait()
+
+    def edge_of(slot):
+        return jnp.concatenate(
+            [hback_recv[slot, p, lev * 8:lev * 8 + 8] for lev in range(16) for p in range(4)], axis=0
+        )
+
+    first = pl.ds(0, 512, stride=4)
+    final = pl.ds(3, 512, stride=4)
+    work[first, :] = work[first, :] + has_down * edge_of(0)
+    work[final, :] = work[final, :] + has_up * edge_of(1)
     adj_copy = pltpu.make_async_copy(work, adj_out, out_sem.at[1])
     adj_copy.start()
 
@@ -396,24 +442,28 @@
     inv_out[...] = jnp.sum(row_recv[...], axis=0)
     levels.wait_send()
     last.wait_send()
-    flow.wait_send()
+    for w in range(4):
+        wave(w, 31 if w == 0 else 32).wait_send()
     final_copy.wait()
     adj_copy.wait()
 
 
 def write_out(*refs):
-    n = len(refs) // 2
-    sems = refs[-1]
-    copies = []
-    for a, b in zip(refs[:n], refs[n:-1]):
+    stages = [], []
+    for a, b, held in zip(refs[:4], refs[4:8], refs[8:12]):
         rows = a.shape[0]
         step = min(rows, 512)
         for at in range(0, rows, step):
-            c = pltpu.make_async_copy(a.at[pl.ds(at, step)], b.at[pl.ds(at, step)], sems.at[len(copies)])
-            c.start()
-            copies.append(c)
-    for c in copies:
+            for n, (src, dst) in enumerate(((a, held), (held, b))):
+                here = pl.ds(at, step)
+                stages[n].append(pltpu.make_async_copy(src.at[here], dst.at[here], refs[12].at[n, len(stages[n])]))
+    for c in stages[0]:
+        c.start()
+    for c, d in zip(*stages):
         c.wait()
+        d.start()
+    for d in stages[1]:
+        d.wait()
 
 
 def rows_of(slab):
@@ -429,7 +479,7 @@
     slab = pltpu.VMEM((ROWS, 128), F32)
     dma = pltpu.SemaphoreType.DMA
     blocks = pltpu.VMEM((N, 16, 128), F32)
-    edge = pltpu.VMEM((2, 512, 128), F32)
+    edge = pltpu.VMEM((2, 4, 128, 128), F32)
     results = pl.pallas_call(
         kernel,
         out_shape=(
@@ -447,7 +497,7 @@
             pltpu.VMEM((N_LEV, N_ROW, 256), F32), pltpu.VMEM((N_LEV, N_ROW, 256), F32),
             pltpu.VMEM((N_ROW, 2, 128), F32), pltpu.VMEM((N_ROW, 2, 128), F32),
             edge, edge, edge, edge, pltpu.VMEM((16, 128), F32),
-            dma((6,)), dma, dma((2,)), dma((4,)), dma((4,)), dma, dma, dma, dma, dma((2,)), dma((2,)), pltpu.SemaphoreType.REGULAR,
+            dma((6,)), dma, dma((2,)), dma((4, 4)), dma((4, 4)), dma, dma, dma((4,)), dma((4,)), dma((2,)), dma((2,)), pltpu.SemaphoreType.REGULAR,
         ],
         compiler_params=pltpu.CompilerParams(
             collective_id=0, has_side_effects=True, vmem_limit_bytes=56 * 1024 * 1024
@@ -463,7 +513,7 @@
         out_shape=tuple(jax.ShapeDtypeStruct(r.shape, r.dtype) for r in results),
         in_specs=[hbm] * 4,
         out_specs=(hbm,) * 4,
-        scratch_shapes=[dma((10,))],
+        scratch_shapes=[pltpu.VMEM(r.shape, r.dtype) for r in results] + [dma((2, 10))],
         name="write_out",
     )(*results)
     adjoint = adjoint.reshape(16, 32, 4, 128).transpose(0, 2, 1, 3).reshape(16, 4, 4096)

time: 155 us -> 87.8 us (0.57)
  Pallas kernels: 154 us -> 87 us
    pallas_call x1, Pallas kernels: 65 us -> 2.44 us  [local(): pl.pallas_call(write_out, out_shape=tuple((jax.ShapeDtypeStruct(r.shape,...]
    pallas_call x1, Pallas kernels: 89.1 us -> 84.5 us  [local(): pl.pallas_call(kernel, out_shape=(jax.ShapeDtypeStruct((ROWS, 128), F32),...]
where the time goes in v3:
time: 87.8 us; the launch traced here: 87.6 us
  Pallas kernels  87 us (99%)
    pallas_call x1, Pallas kernels, local(): pl.pallas_call(kernel, out_shape=(jax.ShapeDtypeStruct((ROWS, 128), F32),...  84.5 us
    pallas_call x1, Pallas kernels, local(): pl.pallas_call(write_out, out_shape=tuple((jax.ShapeDtypeStruct(r.shape,...  2.44 us

profile of v3, /device:TPU:1, one launch (start us, length us, event | category | flops | bytes accessed | tf_op | source)
XLA Modules:
  0.0 87.6 jit_solution(4270249647811511216)
XLA Ops:
  0.6 84.5 %transport.1 = (f32[2048,128]{1,0:T(8,128)}, f32[16,128]{1,0:T(8,128)}, f32[2048,128]{1,0:T(8,128)}, f32[2,128]{1,0:T(2,128)}) custom-call(f32[2048,128]{1,0:T(8,128)} %bitcast.39, f32[2048,128]{1,0:T(8,128)} %bitcast.40, f32[2048,128]{1,0:T(8,128)} %bitcast.41, s32[2048,128]{1,0:T(8,128)} %bitcast.42, s32[2048,128]{1,0:T(8,128)} %bitcast.43, ...), custom_call_target="tpu_custom_call" | custom-call | tf_op jit(solution)/shard_map/transport/pallas_call | solution.py:483
  85.2 2.4 %write_out.1 = (f32[2048,128]{1,0:T(8,128)}, f32[16,128]{1,0:T(8,128)}, f32[2048,128]{1,0:T(8,128)}, f32[2,128]{1,0:T(2,128)}) custom-call(f32[2048,128]{1,0:T(8,128)} %get-tuple-element.12.refs_0_, f32[16,128]{1,0:T(8,128)} %get-tuple-element.13.refs_1_, f32[2048,128]{1,0:T(8,128)} %get-tuple-element.14.refs_2_, f32[2,128]{1,0:T(2,128)} %get-tuple-element.15.refs_3_), custom_call_target="tpu_custom_call" | custom-call | tf_op jit(solution)/shard_map/write_out/pallas_call | solution.py:511

commit v4 on v3

--- a/solution.py
+++ b/solution.py
@@ -15,7 +15,7 @@
 N_ROW = 16
 N = N_LEV * N_ROW
 ROWS = 2048
-REC_TILE = 512
+TILE = 1024
 
 
 def place(d):
@@ -72,9 +72,9 @@
 
 
 def kernel(
-    t_in, cx_in, cy_in, sx_in, sy_in, mat_in, rcell, rlim, scell, sdest, sslot, swt,
+    t_in, cx_in, cy_in, sx_in, sy_in, mat_in, rcell_in, rlim_in, scell_in, sdest_in, sslot_in, swt_in,
     final_out, cross_out, adj_out, inv_out,
-    t, cx, cy, sx, sy, mat, work, cols, field, parts, hot, values, send_a, recv_a, recv_b, level_send, level_recv, row_send, row_recv,
+    t, cx, cy, sx, sy, mat, rcell, rlim, scell, sdest, sslot, swt, cross, inv, work, cols, field, parts, values, send_a, recv_a, recv_b, level_send, level_recv, row_send, row_recv,
     halo_send, halo_recv, hback_send, hback_recv, picked,
     load_sem, own_sem, out_sem, hs_sem, hr_sem, as_sem, ar_sem, bs_sem, br_sem, cs_sem, cr_sem, ready,
 ):
@@ -85,7 +85,11 @@
     down_row = lax.rem(my_row + N_ROW - 1, N_ROW)
 
     loads = []
-    for n, (src, dst) in enumerate(((t_in, t), (cx_in, cx), (cy_in, cy), (sx_in, sx), (sy_in, sy), (mat_in, mat))):
+    inputs = (
+        (t_in, t), (cx_in, cx), (cy_in, cy), (sx_in, sx), (sy_in, sy), (mat_in, mat), (rcell_in, rcell),
+        (rlim_in, rlim), (scell_in, scell), (sdest_in, sdest), (sslot_in, sslot), (swt_in, swt),
+    )
+    for n, (src, dst) in enumerate(inputs):
         c = pltpu.make_async_copy(src, dst, load_sem.at[n])
         c.start()
         loads.append(c)
@@ -217,7 +221,8 @@
             device_id=(my_lev, up_row), device_id_type=MESH,
         )
 
-    loads[5].wait()
+    for c in loads[5:]:
+        c.wait()
     pltpu.make_async_copy(send_a.at[me], recv_a.at[here], own_sem).wait()
     flow = all_of(send_a, recv_a, as_sem, ar_sem)
     flow.wait_recv()
@@ -240,45 +245,48 @@
     final_copy = pltpu.make_async_copy(field, final_out, out_sem.at[0])
     final_copy.start()
 
-    lanes = iota((REC_TILE, 128), 1)
-
-    def column(ref, base):
-        return jnp.concatenate([as_column(ref(base + s)) for s in range(REC_TILE // 128)], axis=0)
-
-    def pick(base, row_of, lane_of, out):
-        rows = column(row_of, base)
-        for k in range(16):
-            hot[:, k * 128:k * 128 + 128] = one_hot(rows == lanes + k * 128)
-        g = dot(hot[...], parts[...], ((1,), (0,)))
-        g = g[:, :128] + g[:, 128:]
-        g = jnp.sum(jnp.where(column(lane_of, base) == lanes, g, 0.0), axis=1, keepdims=True)
-        for s in range(REC_TILE // 128):
+    def column(ref, base, tile):
+        return jnp.concatenate([as_column(ref(base + s)) for s in range(tile // 128)], axis=0)
+
+    def pick(base, tile, row_of, lane_of, out):
+        lanes = iota((tile, 128), 1)
+        rows = column(row_of, base, tile)
+        g = jnp.zeros((tile, 256), F32)
+        for k in range(8):
+            h = jnp.concatenate([one_hot(rows == lanes + (k * 256 + half)) for half in (0, 128)], axis=1)
+            g = g + dot(h, parts[k * 256:k * 256 + 256], ((1,), (0,)))
+        mask = column(lane_of, base, tile) == lanes
+        g = jnp.sum(jnp.where(mask, g[:, :128] + g[:, 128:], 0.0), axis=1, keepdims=True)
+        for s in range(tile // 128):
             out[pl.ds(base + s, 1), :] = as_row(g[s * 128:s * 128 + 128])
-
-    @pl.loop(0, 4)
+        return mask
+
+    @pl.loop(0, 2)
     def _(u):
-        pick(u * 4, lambda s: rcell[pl.ds(s, 1), :] >> 7, lambda s: rcell[pl.ds(s, 1), :] & 127, picked)
+        mask = pick(u * 8, TILE, lambda s: rcell[pl.ds(s, 1), :] >> 7, lambda s: rcell[pl.ds(s, 1), :] & 127, picked)
+        work[pl.ds(pl.multiple_of(u * TILE, TILE), TILE), :] = jnp.where(mask, 1.0, 0.0)
 
     crossing = jax.nn.sigmoid(2.0 * (picked[...] - rlim[...]))
-    cross_out[...] = crossing
+    cross[...] = crossing
+    cross_copy = pltpu.make_async_copy(cross, cross_out, out_sem.at[2])
+    cross_copy.start()
     picked[...] = 2.0 * crossing * (1.0 - crossing)
 
-    @pl.loop(0, 16)
+    @pl.loop(0, 16, unroll=2)
     def _(u):
-        seeds = as_column(picked[pl.ds(u, 1), :])
-        mask = as_column(rcell[pl.ds(u, 1), :] & 127) == tile_lane
-        h, l = halves(jnp.where(mask, seeds, 0.0))
         at = pl.ds(pl.multiple_of(u * 128, 128), 128)
+        h, l = halves(work[at] * as_column(picked[pl.ds(u, 1), :]))
         values[at, 0:128] = h
         values[at, 128:256] = l
 
-    @pl.loop(0, 4)
+    @pl.loop(0, 2)
     def _(u):
-        rows = iota((REC_TILE, 128), 0) + u * REC_TILE
-        for k in range(16):
-            hot[:, k * 128:k * 128 + 128] = one_hot((rcell[k:k + 1, :] >> 7) == rows)
-        g = dot(hot[...], values[...], ((1,), (0,)))
-        work[pl.ds(pl.multiple_of(u * REC_TILE, REC_TILE), REC_TILE), :] = g[:, :128] + g[:, 128:]
+        rows = iota((TILE, 128), 0) + u * TILE
+        g = jnp.zeros((TILE, 256), F32)
+        for k in range(8):
+            h = jnp.concatenate([one_hot((rcell[2 * k + n:2 * k + n + 1, :] >> 7) == rows) for n in (0, 1)], axis=1)
+            g = g + dot(h, values[k * 256:k * 256 + 256], ((1,), (0,)))
+        work[pl.ds(pl.multiple_of(u * TILE, TILE), TILE), :] = g[:, :128] + g[:, 128:]
 
     @pl.loop(0, 32, unroll=4)
     def _(y):
@@ -312,13 +320,6 @@
         for core in range(2):
             send_back(0, j, core)
 
-    @pl.loop(1, 4)
-    def _(w):
-        @pl.loop(0, 16)
-        def _(k):
-            for core in range(2):
-                send_back(w, lax.rem(5 * k + my_row, N_ROW), core)
-
     def wave(w, n):
         return pltpu.make_async_remote_copy(
             send_a.at[pl.ds(0, n)], recv_b.at[pl.ds(0, n)], bs_sem.at[w], br_sem.at[w],
@@ -327,6 +328,13 @@
 
     pltpu.make_async_copy(send_a.at[here], recv_b.at[me], own_sem).wait()
     for w in range(4):
+        if w < 3:
+
+            @pl.loop(0, 16)
+            def _(k):
+                for core in range(2):
+                    send_back(w + 1, lax.rem(5 * k + my_row, N_ROW), core)
+
         wave(w, 31 if w == 0 else 32).wait_recv()
         p = lax.rem(my_y + 4 - w, 4)
 
@@ -393,7 +401,7 @@
         c = scell[pl.ds(s, 1), :]
         return (c >> 14) * 128 + ((c >> 7) & 31) * 4 + ((c >> 12) & 3)
 
-    pick(0, stack_row, lambda s: scell[pl.ds(s, 1), :] & 127, picked)
+    pick(0, 512, stack_row, lambda s: scell[pl.ds(s, 1), :] & 127, picked)
     stack_values = picked[0:4, :] * swt[...]
     partial = jnp.zeros((128, 256), F32)
     wide = iota((128, 256), 1)
@@ -439,13 +447,17 @@
 
     last = all_but_one(row_send, row_recv, N_ROW, 1)
     last.wait_recv()
-    inv_out[...] = jnp.sum(row_recv[...], axis=0)
+    inv[...] = jnp.sum(row_recv[...], axis=0)
+    inv_copy = pltpu.make_async_copy(inv, inv_out, out_sem.at[3])
+    inv_copy.start()
     levels.wait_send()
     last.wait_send()
     for w in range(4):
         wave(w, 31 if w == 0 else 32).wait_send()
     final_copy.wait()
     adj_copy.wait()
+    cross_copy.wait()
+    inv_copy.wait()
 
 
 def write_out(*refs):
@@ -474,7 +486,6 @@
     tracer, courant_x, courant_y, wind_x, wind_y, inverse_diffusion,
     receptor_cell, receptor_limit, stack_cell, stack_dest, stack_slot, stack_weight,
 ):
-    vmem = pl.BlockSpec(memory_space=pltpu.VMEM)
     hbm = pl.BlockSpec(memory_space=pl.ANY)
     slab = pltpu.VMEM((ROWS, 128), F32)
     dma = pltpu.SemaphoreType.DMA
@@ -488,16 +499,18 @@
             jax.ShapeDtypeStruct((ROWS, 128), F32),
             jax.ShapeDtypeStruct((2, 128), F32),
         ),
-        in_specs=[hbm] * 6 + [vmem] * 6,
-        out_specs=(hbm, vmem, hbm, vmem),
+        in_specs=[hbm] * 12,
+        out_specs=(hbm,) * 4,
         scratch_shapes=[
             slab, slab, slab, pltpu.VMEM((ROWS, 128), I32), pltpu.VMEM((ROWS, 128), I32), pltpu.VMEM((32, 128, 128), F32),
-            slab, slab, slab, pltpu.VMEM((ROWS, 256), BF16), pltpu.VMEM((REC_TILE, ROWS), BF16),
+            pltpu.VMEM((16, 128), I32), pltpu.VMEM((16, 128), F32), pltpu.VMEM((4, 128), I32), pltpu.VMEM((4, 128), I32),
+            pltpu.VMEM((4, 128), I32), pltpu.VMEM((4, 128), F32), pltpu.VMEM((16, 128), F32), pltpu.VMEM((2, 128), F32),
+            slab, slab, slab, pltpu.VMEM((ROWS, 256), BF16),
             pltpu.VMEM((ROWS, 256), BF16), blocks, blocks, blocks,
             pltpu.VMEM((N_LEV, N_ROW, 256), F32), pltpu.VMEM((N_LEV, N_ROW, 256), F32),
             pltpu.VMEM((N_ROW, 2, 128), F32), pltpu.VMEM((N_ROW, 2, 128), F32),
             edge, edge, edge, edge, pltpu.VMEM((16, 128), F32),
-            dma((6,)), dma, dma((2,)), dma((4, 4)), dma((4, 4)), dma, dma, dma((4,)), dma((4,)), dma((2,)), dma((2,)), pltpu.SemaphoreType.REGULAR,
+            dma((12,)), dma, dma((4,)), dma((4, 4)), dma((4, 4)), dma, dma, dma((4,)), dma((4,)), dma((2,)), dma((2,)), pltpu.SemaphoreType.REGULAR,
         ],
         compiler_params=pltpu.CompilerParams(
             collective_id=0, has_side_effects=True, vmem_limit_bytes=56 * 1024 * 1024

time: 87.8 us -> 88.6 us (level)
  Pallas kernels: 87 us -> 87.9 us
    pallas_call x1, Pallas kernels: 84.5 us -> 85.4 us  [local(): pl.pallas_call(kernel, out_shape=(jax.ShapeDtypeStruct((ROWS, 128), F32),...]
where the time goes in v4:
time: 88.6 us; the launch traced here: 88.5 us
  Pallas kernels  87.9 us (99%)
    pallas_call x1, Pallas kernels, local(): pl.pallas_call(kernel, out_shape=(jax.ShapeDtypeStruct((ROWS, 128), F32),...  85.4 us
    pallas_call x1, Pallas kernels, local(): pl.pallas_call(write_out, out_shape=tuple((jax.ShapeDtypeStruct(r.shape,...  2.44 us

profile of v4, /device:TPU:1, one launch (start us, length us, event | category | flops | bytes accessed | tf_op | source)
XLA Modules:
  0.0 88.5 jit_solution(16377772717813420071)
XLA Ops:
  0.6 85.4 %transport.1 = (f32[2048,128]{1,0:T(8,128)}, f32[16,128]{1,0:T(8,128)}, f32[2048,128]{1,0:T(8,128)}, f32[2,128]{1,0:T(2,128)}) custom-call(f32[2048,128]{1,0:T(8,128)} %bitcast.39, f32[2048,128]{1,0:T(8,128)} %bitcast.40, f32[2048,128]{1,0:T(8,128)} %bitcast.41, s32[2048,128]{1,0:T(8,128)} %bitcast.42, s32[2048,128]{1,0:T(8,128)} %bitcast.43, ...), custom_call_target="tpu_custom_call" | custom-call | tf_op jit(solution)/shard_map/transport/pallas_call | solution.py:494
  86.1 2.4 %write_out.1 = (f32[2048,128]{1,0:T(8,128)}, f32[16,128]{1,0:T(8,128)}, f32[2048,128]{1,0:T(8,128)}, f32[2,128]{1,0:T(2,128)}) custom-call(f32[2048,128]{1,0:T(8,128)} %get-tuple-element.12.refs_0_, f32[16,128]{1,0:T(8,128)} %get-tuple-element.13.refs_1_, f32[2048,128]{1,0:T(8,128)} %get-tuple-element.14.refs_2_, f32[2,128]{1,0:T(2,128)} %get-tuple-element.15.refs_3_), custom_call_target="tpu_custom_call" | custom-call | tf_op jit(solution)/shard_map/write_out/pallas_call | solution.py:524

commit v5 on v4

--- a/solution.py
+++ b/solution.py
@@ -107,11 +107,26 @@
         pl.semaphore_signal(barrier, inc=1, device_id=other, device_id_type=MESH)
 
     loads[0].wait()
-    my_y = my_lev // 2
+    tile_row = iota((128, 128), 0)
+    tile_lane = iota((128, 128), 1)
+    tile_low = (tile_row & 4) == 0
+
+    def exchange_halves(a, b):
+        return jnp.where(tile_low, a, pltpu.roll(b, 4, 0)), jnp.where(tile_low, pltpu.roll(a, 124, 0), b)
+
     for slot, start in ((0, 3), (1, 0)):
         edge = t[pl.ds(start, 512, stride=4), :].reshape(16, 4, 8, 128)
-        for p in range(4):
-            halo_send[slot, p] = edge[:, p].reshape(128, 128)
+        for n in range(2):
+            a, b = exchange_halves(edge[:, n].reshape(128, 128), edge[:, n + 2].reshape(128, 128))
+            halo_send[slot, 2 * n] = a
+            halo_send[slot, 2 * n + 1] = b
+
+    def piece(w):
+        return 2 * lax.rem(my_lev // 2 + w // 2, 2) + lax.rem(my_lev + w, 2)
+
+    def pair_of(p, n):
+        return 2 * p + lax.rem(n, 2) + 8 * (n // 2)
+
     pl.semaphore_wait(barrier, N_ROW + N_LEV - 2)
 
     @pl.loop(1, N_ROW)
@@ -129,13 +144,11 @@
     @pl.loop(0, 4)
     def _(w):
         for slot in range(2):
-            exchange(halo_send, halo_recv, 0, slot, lax.rem(my_y + w, 4)).start()
+            exchange(halo_send, halo_recv, 0, slot, piece(w)).start()
 
     for c in loads[1:5]:
         c.wait()
 
-    tile_row = iota((128, 128), 0)
-    tile_lane = iota((128, 128), 1)
     strip_row = tile_row & 3
 
     def from_left(v):
@@ -167,8 +180,8 @@
     has_down = jnp.where(my_row > 0, 1.0, 0.0)
     has_up = jnp.where(my_row < N_ROW - 1, 1.0, 0.0)
 
-    def edge_rows(lev, p, r):
-        return pl.ds(lev * 128 + p * 32 + r, 8, stride=4)
+    def edge_rows(lev, half, p, r):
+        return pl.ds(lev * 128 + half * 64 + p * 16 + r, 4, stride=4), pl.ds(lev * 8 + half * 4, 4)
 
     pl.semaphore_wait(ready, N_ROW - 1)
 
@@ -177,20 +190,21 @@
 
     @pl.loop(0, 4)
     def _(w):
-        p = lax.rem(my_y + w, 4)
+        p = piece(w)
         for slot in range(2):
             exchange(halo_send, halo_recv, 0, slot, p).wait()
         for lev in range(16):
-            e = edge_rows(lev, p, 0)
-            v = cx[e, :] * halo_recv[0, p, lev * 8:lev * 8 + 8]
-            work[e, :] = work[e, :] + has_down * jnp.where(sx[e, :] != 0, v, 0.0)
-            e = edge_rows(lev, p, 3)
-            v = cx[e, :] * halo_recv[1, p, lev * 8:lev * 8 + 8]
-            work[e, :] = work[e, :] + has_up * jnp.where(sx[e, :] != 0, 0.0, v)
+            for half in range(2):
+                e, at = edge_rows(lev, half, p, 0)
+                v = cx[e, :] * halo_recv[0, p, at]
+                work[e, :] = work[e, :] + has_down * jnp.where(sx[e, :] != 0, v, 0.0)
+                e, at = edge_rows(lev, half, p, 3)
+                v = cx[e, :] * halo_recv[1, p, at]
+                work[e, :] = work[e, :] + has_up * jnp.where(sx[e, :] != 0, 0.0, v)
 
         @pl.loop(0, 4)
         def _(k):
-            pair = p * 4 + lax.rem(k + me // 8, 4)
+            pair = pair_of(p, lax.rem(k + 2 * (my_lev // 4) + my_row // 8, 4))
             at = pl.multiple_of(pair * 8, 8)
             groups = []
             for group in range(4):
@@ -295,8 +309,8 @@
 
     flow.wait_send()
 
-    def send_back(w, j, core):
-        i = 2 * lax.rem(my_y + w, 4) + core
+    def send_back(w, j, n):
+        i = piece(w) + 4 * lax.rem(my_lev // 4 + n, 2)
         block = j * N_LEV + i
         at_home = (i == my_lev) & (j == my_row)
 
@@ -317,8 +331,15 @@
         v = jnp.concatenate(swap4(v, 1), axis=0).T
         send_a[pl.ds(j * 8, 8)] = v.reshape(8, 16, 128)
 
-        for core in range(2):
-            send_back(0, j, core)
+        for n in range(2):
+            send_back(0, j, n)
+
+    @pl.loop(1, 4)
+    def _(w):
+        @pl.loop(0, 16)
+        def _(k):
+            for n in range(2):
+                send_back(w, lax.rem(5 * k + my_row, N_ROW), n)
 
     def wave(w, n):
         return pltpu.make_async_remote_copy(
@@ -328,19 +349,12 @@
 
     pltpu.make_async_copy(send_a.at[here], recv_b.at[me], own_sem).wait()
     for w in range(4):
-        if w < 3:
-
-            @pl.loop(0, 16)
-            def _(k):
-                for core in range(2):
-                    send_back(w + 1, lax.rem(5 * k + my_row, N_ROW), core)
-
         wave(w, 31 if w == 0 else 32).wait_recv()
-        p = lax.rem(my_y + 4 - w, 4)
+        p = piece(w)
 
         @pl.loop(0, 4)
         def _(k):
-            at = pl.multiple_of((p * 4 + k) * 8, 8)
+            at = pl.multiple_of(pair_of(p, k) * 8, 8)
             for half in range(2):
                 va, vb = [], []
                 for q in range(4):
@@ -353,10 +367,11 @@
                         t[pl.ds(pl.multiple_of((group * 4 + g) * 128 + at, 8), 8), :] = u
 
         for lev in range(16):
-            e = edge_rows(lev, p, 3)
-            hback_send[0, p, lev * 8:lev * 8 + 8] = jnp.where(sx[e, :] != 0, 0.0, cx[e, :] * t[e, :])
-            e = edge_rows(lev, p, 0)
-            hback_send[1, p, lev * 8:lev * 8 + 8] = jnp.where(sx[e, :] != 0, cx[e, :] * t[e, :], 0.0)
+            for half in range(2):
+                e, at = edge_rows(lev, half, p, 3)
+                hback_send[0, p, at] = jnp.where(sx[e, :] != 0, 0.0, cx[e, :] * t[e, :])
+                e, at = edge_rows(lev, half, p, 0)
+                hback_send[1, p, at] = jnp.where(sx[e, :] != 0, cx[e, :] * t[e, :], 0.0)
         for slot in range(2):
             exchange(hback_send, hback_recv, 2, slot, p).start()
 
@@ -379,9 +394,10 @@
             exchange(hback_send, hback_recv, 2, slot, p).wait()
 
     def edge_of(slot):
-        return jnp.concatenate(
-            [hback_recv[slot, p, lev * 8:lev * 8 + 8] for lev in range(16) for p in range(4)], axis=0
-        )
+        v = exchange_halves(hback_recv[slot, 0], hback_recv[slot, 1])
+        u = exchange_halves(hback_recv[slot, 2], hback_recv[slot, 3])
+        v = (v[0], u[0], v[1], u[1])
+        return jnp.concatenate([x[lev * 8:lev * 8 + 8] for lev in range(16) for x in v], axis=0)
 
     first = pl.ds(0, 512, stride=4)
     final = pl.ds(3, 512, stride=4)

time: 88.6 us -> 79.8 us (0.901)
  Pallas kernels: 87.9 us -> 79 us
    pallas_call x1, Pallas kernels: 85.4 us -> 76.6 us  [local(): pl.pallas_call(kernel, out_shape=(jax.ShapeDtypeStruct((ROWS, 128), F32),...]
where the time goes in v5:
time: 79.8 us; the launch traced here: 79.7 us
  Pallas kernels  79 us (99%)
    pallas_call x1, Pallas kernels, local(): pl.pallas_call(kernel, out_shape=(jax.ShapeDtypeStruct((ROWS, 128), F32),...  76.6 us
    pallas_call x1, Pallas kernels, local(): pl.pallas_call(write_out, out_shape=tuple((jax.ShapeDtypeStruct(r.shape,...  2.44 us

profile of v5, /device:TPU:1, one launch (start us, length us, event | category | flops | bytes accessed | tf_op | source)
XLA Modules:
  0.0 79.7 jit_solution(3065476361251876611)
XLA Ops:
  0.6 76.6 %transport.1 = (f32[2048,128]{1,0:T(8,128)}, f32[16,128]{1,0:T(8,128)}, f32[2048,128]{1,0:T(8,128)}, f32[2,128]{1,0:T(2,128)}) custom-call(f32[2048,128]{1,0:T(8,128)} %bitcast.39, f32[2048,128]{1,0:T(8,128)} %bitcast.40, f32[2048,128]{1,0:T(8,128)} %bitcast.41, s32[2048,128]{1,0:T(8,128)} %bitcast.42, s32[2048,128]{1,0:T(8,128)} %bitcast.43, ...), custom_call_target="tpu_custom_call" | custom-call | tf_op jit(solution)/shard_map/transport/pallas_call | solution.py:510
  77.2 2.4 %write_out.1 = (f32[2048,128]{1,0:T(8,128)}, f32[16,128]{1,0:T(8,128)}, f32[2048,128]{1,0:T(8,128)}, f32[2,128]{1,0:T(2,128)}) custom-call(f32[2048,128]{1,0:T(8,128)} %get-tuple-element.12.refs_0_, f32[16,128]{1,0:T(8,128)} %get-tuple-element.13.refs_1_, f32[2048,128]{1,0:T(8,128)} %get-tuple-element.14.refs_2_, f32[2,128]{1,0:T(2,128)} %get-tuple-element.15.refs_3_), custom_call_target="tpu_custom_call" | custom-call | tf_op jit(solution)/shard_map/write_out/pallas_call | solution.py:540

commit v6 on v5

--- a/solution.py
+++ b/solution.py
@@ -15,6 +15,7 @@
 N_ROW = 16
 N = N_LEV * N_ROW
 ROWS = 2048
+PITCH = 40
 TILE = 1024
 
 
@@ -60,10 +61,9 @@
     return lax.dot_general(a, b, (dims, ((), ())), preferred_element_type=F32)
 
 
-def dot_split(a, b, dims):
+def dot_split(a, b):
     n = a.shape[0]
-    side = 0 if dims[1] == (1,) else 1
-    g = dot(jnp.concatenate(halves(a), axis=0), jnp.concatenate(halves(b), axis=side), dims)
+    g = dot(jnp.concatenate(halves(a), axis=0), b, ((1,), (0,)))
     return (g[:n, :128] + g[n:, :128]) + (g[:n, 128:] + g[n:, 128:])
 
 
@@ -74,12 +74,14 @@
 def kernel(
     t_in, cx_in, cy_in, sx_in, sy_in, mat_in, rcell_in, rlim_in, scell_in, sdest_in, sslot_in, swt_in,
     final_out, cross_out, adj_out, inv_out,
-    t, cx, cy, sx, sy, mat, rcell, rlim, scell, sdest, sslot, swt, cross, inv, work, cols, field, parts, values, send_a, recv_a, recv_b, level_send, level_recv, row_send, row_recv,
+    t, cx, cy, sx, sy, mat, rcell, rlim, scell, sdest, sslot, swt, cross, inv,
+    mat_fwd, mat_back, hot, hot_turned, work, cols, field, parts, values, send_a, recv_a, recv_b, owner_send, owner_recv, core_send, core_recv,
     halo_send, halo_recv, hback_send, hback_recv, picked,
-    load_sem, own_sem, out_sem, hs_sem, hr_sem, as_sem, ar_sem, bs_sem, br_sem, cs_sem, cr_sem, ready,
+    load_sem, own_sem, out_sem, hs_sem, hr_sem, as_sem, ar_sem, bs_sem, br_sem, cs_sem, cr_sem, ps_sem, pr_sem, ready,
 ):
     my_lev = lax.axis_index("lev")
     my_row = lax.axis_index("row")
+    my_y = my_lev // 2
     me = my_lev * N_ROW + my_row
     up_row = lax.rem(my_row + 1, N_ROW)
     down_row = lax.rem(my_row + N_ROW - 1, N_ROW)
@@ -204,7 +206,7 @@
 
         @pl.loop(0, 4)
         def _(k):
-            pair = pair_of(p, lax.rem(k + 2 * (my_lev // 4) + my_row // 8, 4))
+            pair = pair_of(p, lax.rem(3 + 3 * k + 2 * (my_lev // 4) + my_row // 8, 4))
             at = pl.multiple_of(pair * 8, 8)
             groups = []
             for group in range(4):
@@ -218,14 +220,15 @@
 
             @pl.loop(0, 8)
             def _(e):
-                @pl.when(w + k + e > 0)
+                other = at + lax.rem(6 + 7 * e + me, 8)
+
+                @pl.when(other != me)
                 def _():
-                    other = at + lax.rem(e + me, 8)
                     pltpu.make_async_remote_copy(
                         send_a.at[other], recv_a.at[here], as_sem, ar_sem, device_id=place(other), device_id_type=MESH
                     ).start()
 
-                @pl.when(w + k + e == 0)
+                @pl.when(other == me)
                 def _():
                     pltpu.make_async_copy(send_a.at[me], recv_a.at[here], own_sem).start()
 
@@ -237,6 +240,27 @@
 
     for c in loads[5:]:
         c.wait()
+
+    @pl.loop(0, 32, unroll=4)
+    def _(y):
+        mat_back[y] = jnp.concatenate(halves(mat[y]), axis=1)
+        mat_fwd[y] = jnp.concatenate(halves(mat[y].T), axis=1)
+
+    @pl.loop(0, 16, unroll=2)
+    def _(u):
+        at = pl.ds(pl.multiple_of(u * 128, 128), 128)
+        t[at] = jnp.where(as_column(rcell[pl.ds(u, 1), :] & 127) == tile_lane, 1.0, 0.0)
+        rows = as_column(rcell[pl.ds(u, 1), :] >> 7)
+        for k in range(16):
+            hot[at, k * 128:k * 128 + 128] = one_hot(rows == tile_lane + k * 128)
+
+    @pl.loop(0, 16, unroll=2)
+    def _(u):
+        at = pl.ds(pl.multiple_of(u * 128, 128), 128)
+        rows = tile_row + u * 128
+        for k in range(16):
+            hot_turned[at, k * 128:k * 128 + 128] = one_hot((rcell[k:k + 1, :] >> 7) == rows)
+
     pltpu.make_async_copy(send_a.at[me], recv_a.at[here], own_sem).wait()
     flow = all_of(send_a, recv_a, as_sem, ar_sem)
     flow.wait_recv()
@@ -245,11 +269,11 @@
     def _(j):
         v = recv_a[pl.ds(j * 8, 8)].reshape(128, 128).T
         for r, u in enumerate(swap4([v[g * 32:g * 32 + 32] for g in range(4)], 1)):
-            cols[pl.ds(pl.multiple_of(j * 128 + r * 32, 32), 32), :] = u
+            cols[pl.ds(pl.multiple_of((j * 4 + r) * PITCH, 8), 32), :] = u
 
     @pl.loop(0, 32, unroll=4)
     def _(y):
-        v = dot_split(cols[pl.ds(y, 64, stride=32), :], mat[y], ((1,), (1,)))
+        v = dot_split(cols[pl.ds(y, 64, stride=PITCH), :], mat_fwd[y])
         at = pl.ds(pl.multiple_of(y * 64, 64), 64)
         field[at] = v
         h, l = halves(v)
@@ -259,26 +283,21 @@
     final_copy = pltpu.make_async_copy(field, final_out, out_sem.at[0])
     final_copy.start()
 
-    def column(ref, base, tile):
-        return jnp.concatenate([as_column(ref(base + s)) for s in range(tile // 128)], axis=0)
-
-    def pick(base, tile, row_of, lane_of, out):
-        lanes = iota((tile, 128), 1)
-        rows = column(row_of, base, tile)
-        g = jnp.zeros((tile, 256), F32)
+    def product(a, b):
+        g = jnp.zeros((a.shape[0], 256), F32)
         for k in range(8):
-            h = jnp.concatenate([one_hot(rows == lanes + (k * 256 + half)) for half in (0, 128)], axis=1)
-            g = g + dot(h, parts[k * 256:k * 256 + 256], ((1,), (0,)))
-        mask = column(lane_of, base, tile) == lanes
-        g = jnp.sum(jnp.where(mask, g[:, :128] + g[:, 128:], 0.0), axis=1, keepdims=True)
-        for s in range(tile // 128):
+            g = g + dot(a[:, k * 256:k * 256 + 256], b[k * 256:k * 256 + 256], ((1,), (0,)))
+        return g[:, :128] + g[:, 128:]
+
+    def place_in_rows(g, mask, base, out):
+        g = jnp.sum(jnp.where(mask, g, 0.0), axis=1, keepdims=True)
+        for s in range(g.shape[0] // 128):
             out[pl.ds(base + s, 1), :] = as_row(g[s * 128:s * 128 + 128])
-        return mask
 
     @pl.loop(0, 2)
     def _(u):
-        mask = pick(u * 8, TILE, lambda s: rcell[pl.ds(s, 1), :] >> 7, lambda s: rcell[pl.ds(s, 1), :] & 127, picked)
-        work[pl.ds(pl.multiple_of(u * TILE, TILE), TILE), :] = jnp.where(mask, 1.0, 0.0)
+        at = pl.ds(pl.multiple_of(u * TILE, TILE), TILE)
+        place_in_rows(product(hot.at[at], parts), t[at] != 0.0, u * 8, picked)
 
     crossing = jax.nn.sigmoid(2.0 * (picked[...] - rlim[...]))
     cross[...] = crossing
@@ -289,28 +308,27 @@
     @pl.loop(0, 16, unroll=2)
     def _(u):
         at = pl.ds(pl.multiple_of(u * 128, 128), 128)
-        h, l = halves(work[at] * as_column(picked[pl.ds(u, 1), :]))
+        h, l = halves(t[at] * as_column(picked[pl.ds(u, 1), :]))
         values[at, 0:128] = h
         values[at, 128:256] = l
 
     @pl.loop(0, 2)
     def _(u):
-        rows = iota((TILE, 128), 0) + u * TILE
-        g = jnp.zeros((TILE, 256), F32)
-        for k in range(8):
-            h = jnp.concatenate([one_hot((rcell[2 * k + n:2 * k + n + 1, :] >> 7) == rows) for n in (0, 1)], axis=1)
-            g = g + dot(h, values[k * 256:k * 256 + 256], ((1,), (0,)))
-        work[pl.ds(pl.multiple_of(u * TILE, TILE), TILE), :] = g[:, :128] + g[:, 128:]
+        at = pl.ds(pl.multiple_of(u * TILE, TILE), TILE)
+        work[at] = product(hot_turned.at[at], values)
 
     @pl.loop(0, 32, unroll=4)
     def _(y):
         at = pl.ds(pl.multiple_of(y * 64, 64), 64)
-        cols[pl.ds(y, 64, stride=32), :] = dot_split(work[at], mat[y], ((1,), (0,)))
+        cols[pl.ds(y, 64, stride=PITCH), :] = dot_split(work[at], mat_back[y])
 
     flow.wait_send()
 
+    def far_strip(k):
+        return 4 * lax.rem(my_row // 4 + 2 + 3 * (k // 4), 4) + lax.rem(my_row + 2 + 3 * k, 4)
+
     def send_back(w, j, n):
-        i = piece(w) + 4 * lax.rem(my_lev // 4 + n, 2)
+        i = piece(w) + 4 * lax.rem(my_lev // 4 + 1 + n, 2)
         block = j * N_LEV + i
         at_home = (i == my_lev) & (j == my_row)
 
@@ -326,8 +344,8 @@
 
     @pl.loop(0, 16)
     def _(k):
-        j = lax.rem(5 * k + my_row, N_ROW)
-        v = [cols[pl.ds(pl.multiple_of(j * 128 + r * 32, 32), 32), :] for r in range(4)]
+        j = far_strip(k)
+        v = [cols[pl.ds(pl.multiple_of((j * 4 + r) * PITCH, 8), 32), :] for r in range(4)]
         v = jnp.concatenate(swap4(v, 1), axis=0).T
         send_a[pl.ds(j * 8, 8)] = v.reshape(8, 16, 128)
 
@@ -339,7 +357,15 @@
         @pl.loop(0, 16)
         def _(k):
             for n in range(2):
-                send_back(w, lax.rem(5 * k + my_row, N_ROW), n)
+                send_back(w, far_strip(k), n)
+
+    for s in range(4):
+        c = scell[s:s + 1, :]
+        at = pl.ds(s * 128, 128)
+        cols[at] = jnp.where(as_column(c & 127) == tile_lane, 1.0, 0.0)
+        rows = as_column((c >> 14) * 128 + ((c >> 7) & 31) * 4 + ((c >> 12) & 3))
+        for k in range(16):
+            hot[at, k * 128:k * 128 + 128] = one_hot(rows == tile_lane + k * 128)
 
     def wave(w, n):
         return pltpu.make_async_remote_copy(
@@ -413,11 +439,7 @@
         parts[at, 0:128] = h
         parts[at, 128:256] = l
 
-    def stack_row(s):
-        c = scell[pl.ds(s, 1), :]
-        return (c >> 14) * 128 + ((c >> 7) & 31) * 4 + ((c >> 12) & 3)
-
-    pick(0, 512, stack_row, lambda s: scell[pl.ds(s, 1), :] & 127, picked)
+    place_in_rows(product(hot.at[pl.ds(0, 512)], parts), cols[0:512] != 0.0, 0, picked)
     stack_values = picked[0:4, :] * swt[...]
     partial = jnp.zeros((128, 256), F32)
     wide = iota((128, 256), 1)
@@ -429,44 +451,43 @@
         amount = jnp.concatenate([amount, amount], axis=1)
         h, l = halves(jnp.where(slot == wide, amount, 0.0))
         partial = partial + (dot(owner, h, ((1,), (0,))) + dot(owner, l, ((1,), (0,))))
-    level_send[...] = partial.reshape(N_LEV, N_ROW, 256)
-    level_recv[my_lev] = level_send[my_lev]
-
-    @pl.loop(1, N_LEV)
-    def _(k):
-        other = lax.rem(my_lev + k, N_LEV)
-        pltpu.make_async_remote_copy(
-            level_send.at[other], level_recv.at[my_lev], cs_sem.at[0], cr_sem.at[0],
-            device_id=(other, my_row), device_id_type=MESH,
-        ).start()
-
-    def all_but_one(send, recv, n, slot):
-        return pltpu.make_async_remote_copy(
-            send.at[pl.ds(0, n - 1)], recv.at[pl.ds(0, n - 1)], cs_sem.at[slot], cr_sem.at[slot],
-            device_id=(my_lev, up_row), device_id_type=MESH,
-        )
-
-    levels = all_but_one(level_send, level_recv, N_LEV, 0)
-    levels.wait_recv()
-    total = jnp.sum(level_recv[...], axis=0)
-    row_send[:, 0, :] = total[:, :128]
-    row_send[:, 1, :] = total[:, 128:]
-    row_recv[my_row] = row_send[my_row]
-
-    @pl.loop(1, N_ROW)
-    def _(k):
-        other = lax.rem(my_row + k, N_ROW)
-        pltpu.make_async_remote_copy(
-            row_send.at[other], row_recv.at[my_row], cs_sem.at[1], cr_sem.at[1],
-            device_id=(my_lev, other), device_id_type=MESH,
-        ).start()
-
-    last = all_but_one(row_send, row_recv, N_ROW, 1)
+    core = lax.rem(my_lev, 2)
+    core_send[...] = partial.reshape(4, 2, N_ROW, 256)
+    other_core = (2 * my_y + 1 - core, my_row)
+    swap = pltpu.make_async_remote_copy(
+        core_send.at[:, 1 - core], core_recv, ps_sem, pr_sem, device_id=other_core, device_id_type=MESH
+    )
+    swap.start()
+    swap.wait_recv()
+    total = (core_send[:, core] + core_recv[...]).reshape(64, 256)
+    owner_send[:, 0, :] = total[:, :128]
+    owner_send[:, 1, :] = total[:, 128:]
+    here = my_y * N_ROW + my_row
+    owner_recv[here] = owner_send[here]
+
+    for dy in (2, 1, 3, 0):
+        y = lax.rem(my_y + dy, 4)
+
+        @pl.loop(0, 16)
+        def _(k):
+            row = far_strip(k)
+
+            @pl.when(y * N_ROW + row != here)
+            def _():
+                pltpu.make_async_remote_copy(
+                    owner_send.at[y * N_ROW + row], owner_recv.at[here], cs_sem, cr_sem,
+                    device_id=(2 * y + core, row), device_id_type=MESH,
+                ).start()
+
+    last = pltpu.make_async_remote_copy(
+        owner_send.at[pl.ds(0, 63)], owner_recv.at[pl.ds(0, 63)], cs_sem, cr_sem,
+        device_id=other_core, device_id_type=MESH,
+    )
     last.wait_recv()
-    inv[...] = jnp.sum(row_recv[...], axis=0)
+    inv[...] = jnp.sum(owner_recv[...], axis=0)
     inv_copy = pltpu.make_async_copy(inv, inv_out, out_sem.at[3])
     inv_copy.start()
-    levels.wait_send()
+    swap.wait_send()
     last.wait_send()
     for w in range(4):
         wave(w, 31 if w == 0 else 32).wait_send()
@@ -521,12 +542,14 @@
             slab, slab, slab, pltpu.VMEM((ROWS, 128), I32), pltpu.VMEM((ROWS, 128), I32), pltpu.VMEM((32, 128, 128), F32),
             pltpu.VMEM((16, 128), I32), pltpu.VMEM((16, 128), F32), pltpu.VMEM((4, 128), I32), pltpu.VMEM((4, 128), I32),
             pltpu.VMEM((4, 128), I32), pltpu.VMEM((4, 128), F32), pltpu.VMEM((16, 128), F32), pltpu.VMEM((2, 128), F32),
-            slab, slab, slab, pltpu.VMEM((ROWS, 256), BF16),
+            pltpu.VMEM((32, 128, 256), BF16), pltpu.VMEM((32, 128, 256), BF16),
+            pltpu.VMEM((ROWS, ROWS), BF16), pltpu.VMEM((ROWS, ROWS), BF16),
+            slab, pltpu.VMEM((64 * PITCH, 128), F32), slab, pltpu.VMEM((ROWS, 256), BF16),
             pltpu.VMEM((ROWS, 256), BF16), blocks, blocks, blocks,
-            pltpu.VMEM((N_LEV, N_ROW, 256), F32), pltpu.VMEM((N_LEV, N_ROW, 256), F32),
-            pltpu.VMEM((N_ROW, 2, 128), F32), pltpu.VMEM((N_ROW, 2, 128), F32),
+            pltpu.VMEM((64, 2, 128), F32), pltpu.VMEM((64, 2, 128), F32),
+            pltpu.VMEM((4, 2, N_ROW, 256), F32), pltpu.VMEM((4, N_ROW, 256), F32),
             edge, edge, edge, edge, pltpu.VMEM((16, 128), F32),
-            dma((12,)), dma, dma((4,)), dma((4, 4)), dma((4, 4)), dma, dma, dma((4,)), dma((4,)), dma((2,)), dma((2,)), pltpu.SemaphoreType.REGULAR,
+            dma((12,)), dma, dma((4,)), dma((4, 4)), dma((4, 4)), dma, dma, dma((4,)), dma((4,)), dma, dma, dma, dma, pltpu.SemaphoreType.REGULAR,
         ],
         compiler_params=pltpu.CompilerParams(
             collective_id=0, has_side_effects=True, vmem_limit_bytes=56 * 1024 * 1024

time: 79.8 us -> 77.8 us (0.975)
  Pallas kernels: 79 us -> 77.1 us
    pallas_call x1, Pallas kernels: 76.6 us -> 74.6 us  [local(): pl.pallas_call(kernel, out_shape=(jax.ShapeDtypeStruct((ROWS, 128), F32),...]
where the time goes in v6:
time: 77.8 us; the launch traced here: 77.7 us
  Pallas kernels  77.1 us (99%)
    pallas_call x1, Pallas kernels, local(): pl.pallas_call(kernel, out_shape=(jax.ShapeDtypeStruct((ROWS, 128), F32),...  74.6 us
    pallas_call x1, Pallas kernels, local(): pl.pallas_call(write_out, out_shape=tuple((jax.ShapeDtypeStruct(r.shape,...  2.44 us

profile of v6, /device:TPU:1, one launch (start us, length us, event | category | flops | bytes accessed | tf_op | source)
XLA Modules:
  0.0 77.7 jit_solution(3644112690529270222)
XLA Ops:
  0.6 74.6 %transport.1 = (f32[2048,128]{1,0:T(8,128)}, f32[16,128]{1,0:T(8,128)}, f32[2048,128]{1,0:T(8,128)}, f32[2,128]{1,0:T(2,128)}) custom-call(f32[2048,128]{1,0:T(8,128)} %bitcast.39, f32[2048,128]{1,0:T(8,128)} %bitcast.40, f32[2048,128]{1,0:T(8,128)} %bitcast.41, s32[2048,128]{1,0:T(8,128)} %bitcast.42, s32[2048,128]{1,0:T(8,128)} %bitcast.43, ...), custom_call_target="tpu_custom_call" | custom-call | tf_op jit(solution)/shard_map/transport/pallas_call | solution.py:531
  75.3 2.4 %write_out.1 = (f32[2048,128]{1,0:T(8,128)}, f32[16,128]{1,0:T(8,128)}, f32[2048,128]{1,0:T(8,128)}, f32[2,128]{1,0:T(2,128)}) custom-call(f32[2048,128]{1,0:T(8,128)} %get-tuple-element.12.refs_0_, f32[16,128]{1,0:T(8,128)} %get-tuple-element.13.refs_1_, f32[2048,128]{1,0:T(8,128)} %get-tuple-element.14.refs_2_, f32[2,128]{1,0:T(2,128)} %get-tuple-element.15.refs_3_), custom_call_target="tpu_custom_call" | custom-call | tf_op jit(solution)/shard_map/write_out/pallas_call | solution.py:563

commit v7 on v6

--- a/solution.py
+++ b/solution.py
@@ -265,13 +265,13 @@
     flow = all_of(send_a, recv_a, as_sem, ar_sem)
     flow.wait_recv()
 
-    @pl.loop(0, 16, unroll=2)
+    @pl.loop(0, 16, unroll=4)
     def _(j):
         v = recv_a[pl.ds(j * 8, 8)].reshape(128, 128).T
         for r, u in enumerate(swap4([v[g * 32:g * 32 + 32] for g in range(4)], 1)):
             cols[pl.ds(pl.multiple_of((j * 4 + r) * PITCH, 8), 32), :] = u
 
-    @pl.loop(0, 32, unroll=4)
+    @pl.loop(0, 32, unroll=8)
     def _(y):
         v = dot_split(cols[pl.ds(y, 64, stride=PITCH), :], mat_fwd[y])
         at = pl.ds(pl.multiple_of(y * 64, 64), 64)
@@ -317,7 +317,7 @@
         at = pl.ds(pl.multiple_of(u * TILE, TILE), TILE)
         work[at] = product(hot_turned.at[at], values)
 
-    @pl.loop(0, 32, unroll=4)
+    @pl.loop(0, 32, unroll=8)
     def _(y):
         at = pl.ds(pl.multiple_of(y * 64, 64), 64)
         cols[pl.ds(y, 64, stride=PITCH), :] = dot_split(work[at], mat_back[y])
@@ -378,7 +378,7 @@
         wave(w, 31 if w == 0 else 32).wait_recv()
         p = piece(w)
 
-        @pl.loop(0, 4)
+        @pl.loop(0, 4, unroll=2)
         def _(k):
             at = pl.multiple_of(pair_of(p, k) * 8, 8)
             for half in range(2):

time: 77.8 us -> 76.1 us (0.978)
  Pallas kernels: 77.1 us -> 75.3 us
    pallas_call x1, Pallas kernels: 74.6 us -> 72.8 us  [local(): pl.pallas_call(kernel, out_shape=(jax.ShapeDtypeStruct((ROWS, 128), F32),...]
where the time goes in v7:
time: 76.1 us; the launch traced here: 75.9 us
  Pallas kernels  75.3 us (99%)
    pallas_call x1, Pallas kernels, local(): pl.pallas_call(kernel, out_shape=(jax.ShapeDtypeStruct((ROWS, 128), F32),...  72.8 us
    pallas_call x1, Pallas kernels, local(): pl.pallas_call(write_out, out_shape=tuple((jax.ShapeDtypeStruct(r.shape,...  2.44 us

profile of v7, /device:TPU:1, one launch (start us, length us, event | category | flops | bytes accessed | tf_op | source)
XLA Modules:
  0.0 75.9 jit_solution(14069174390610379071)
XLA Ops:
  0.6 72.8 %transport.1 = (f32[2048,128]{1,0:T(8,128)}, f32[16,128]{1,0:T(8,128)}, f32[2048,128]{1,0:T(8,128)}, f32[2,128]{1,0:T(2,128)}) custom-call(f32[2048,128]{1,0:T(8,128)} %bitcast.39, f32[2048,128]{1,0:T(8,128)} %bitcast.40, f32[2048,128]{1,0:T(8,128)} %bitcast.41, s32[2048,128]{1,0:T(8,128)} %bitcast.42, s32[2048,128]{1,0:T(8,128)} %bitcast.43, ...), custom_call_target="tpu_custom_call" | custom-call | tf_op jit(solution)/shard_map/transport/pallas_call | solution.py:531
  73.5 2.4 %write_out.1 = (f32[2048,128]{1,0:T(8,128)}, f32[16,128]{1,0:T(8,128)}, f32[2048,128]{1,0:T(8,128)}, f32[2,128]{1,0:T(2,128)}) custom-call(f32[2048,128]{1,0:T(8,128)} %get-tuple-element.12.refs_0_, f32[16,128]{1,0:T(8,128)} %get-tuple-element.13.refs_1_, f32[2048,128]{1,0:T(8,128)} %get-tuple-element.14.refs_2_, f32[2,128]{1,0:T(2,128)} %get-tuple-element.15.refs_3_), custom_call_target="tpu_custom_call" | custom-call | tf_op jit(solution)/shard_map/write_out/pallas_call | solution.py:563
